TPU v7x, 512 devices: a whole 4x8x8 slice. The times are simulated.
512 devices in a mesh: band: 64 (over z, x, core), lon: 8 (over y).
Axes of the slice: x: 4, y: 8, z: 8, core: 2. Of those that a mesh axis runs over, the one named last changes fastest.
Arguments:
- spectral_in: float32 [512, 32, 641], P(('band', 'lon')), may hold values from -6 to 6
- leg_synthesis: float32 [512, 641, 640], P(('band', 'lon')), may hold values from -0.25 to 0.25
- leg_analysis: float32 [512, 640, 641], P(('band', 'lon')), may hold values from -0.15625 to 0.15625
- slot_pair: int32 [512], replicated, may hold values from 0 to 320, as said below
- departure_cells: int32 [1280, 2560], P('band'), may hold values from 0 to 3
- departure_frac: float32 [1280, 2560], P('band'), may hold values from 0 to 1
Outputs:
- spectral_out: float32 [512, 32, 641], P(('band', 'lon'))
Inputs may be any that keep to these rules, and one draw needn't show every extreme that they name: `slot_pair`: every pair 0 to 319 stands in exactly one slot; the value 320 marks an empty slot; all slots of at least one index of band hold pairs.
All inputs are finite; a program needn't handle non-finite values.
Results may differ from a plain program's by a relative error of at most 0.0003.
Values sent between devices are 32-bit elements; how exact they have to be, the bound alone decides.
No kernel may reach another device: no remote copies, remote signals or barrier semaphores. Data moves between devices by JAX's collectives and lax.ppermute only.
A program may use at most 64 MiB of HBM per device.

v0:
```python
import math

import jax
import jax.numpy as jnp
from jax import lax
from jax.sharding import PartitionSpec as P

WAVES = 640
PAIRS = 320
ROWS = 641
NLON = 2560
REACH = 4


def from_behind(value, axis, steps):
    count = lax.axis_size(axis)
    pairs = [(source, (source + steps) % count) for source in range(count)]
    return lax.ppermute(value, axis, pairs)


def row_masks(pair_ids):
    row_index = jnp.arange(ROWS, dtype=jnp.int32)[None, :]
    split_row = (WAVES - pair_ids)[:, None]
    upper_part = row_index < split_row
    parity = jnp.where(upper_part, row_index, row_index - split_row) % 2
    even_rows = (parity == 0).astype(jnp.float32)
    active = (pair_ids < PAIRS)[:, None]
    first_wave = jnp.logical_and(upper_part, active).astype(jnp.float32)
    second_wave = jnp.logical_and(jnp.logical_not(upper_part), active).astype(jnp.float32)
    return (first_wave, second_wave, even_rows)


def inverse_legendre(spectrum, table, pair_ids):
    first_wave, second_wave, even_rows = row_masks(pair_ids)
    row_signs = 2.0 * even_rows - 1.0
    weights = jnp.stack(
        [first_wave, first_wave * row_signs, second_wave, second_wave * row_signs], axis=1
    )
    masked = spectrum[:, None, :, :] * weights[:, :, None, :]
    product = jnp.einsum("sacr,srh->sach", masked, table, precision=lax.Precision.HIGHEST)
    northern = product[:, 0::2]
    southern = product[:, 1::2]
    return jnp.concatenate([northern, jnp.flip(southern, axis=3)], axis=3)


def direct_legendre(fourier, table, pair_ids):
    half_lat = fourier.shape[3] // 2
    northern = fourier[..., :half_lat]
    southern = jnp.flip(fourier[..., half_lat:], axis=3)
    stacked = jnp.stack([northern + southern, northern - southern], axis=2)
    stacked = stacked.reshape(fourier.shape[0], 4, fourier.shape[2], half_lat)
    product = jnp.einsum("sach,shr->sacr", stacked, table, precision=lax.Precision.HIGHEST)
    first_wave, second_wave, even_rows = row_masks(pair_ids)
    odd_rows = 1.0 - even_rows
    weights = jnp.stack(
        [
            first_wave * even_rows,
            first_wave * odd_rows,
            second_wave * even_rows,
            second_wave * odd_rows,
        ],
        axis=1,
    )
    return jnp.sum(product * weights[:, :, None, :], axis=1)


def slot_waves(slot_pair, row_ids, lon_count, slot_dev):
    columns = slot_pair.shape[0] // lon_count
    column = row_ids // columns
    inner_index = row_ids % columns
    owner_band = inner_index // slot_dev
    seat_index = inner_index % slot_dev
    slot_index = (owner_band * lon_count + column) * slot_dev + seat_index
    pair_ids = jnp.take(slot_pair, slot_index)
    wave_ids = jnp.stack([pair_ids, WAVES - 1 - pair_ids], axis=1)
    active = (pair_ids < PAIRS).astype(jnp.float32)[:, None]
    return (wave_ids, active)


def wave_basis(wave_ids, active, longitudes, synthesis):
    phases = wave_ids[..., None] * longitudes % NLON
    angles = phases.astype(jnp.float32) * (2.0 * math.pi / NLON)
    if synthesis:
        factor = jnp.where(wave_ids == 0, 1.0, 2.0) * active
    else:
        factor = jnp.zeros(wave_ids.shape, jnp.float32) + active * (1.0 / NLON)
    basis = jnp.stack([jnp.cos(angles), -jnp.sin(angles)], axis=-2) * factor[..., None, None]
    return basis.reshape(-1, longitudes.shape[0])


def per_device(
    spectral_in, leg_synthesis, leg_analysis, slot_pair, departure_cells, departure_frac
):
    band_count = lax.axis_size("band")
    lon_count = lax.axis_size("lon")
    lon_index = lax.axis_index("lon")
    slot_dev = spectral_in.shape[0]
    doubled = spectral_in.shape[1]
    variables = doubled // 2
    lat_band = departure_cells.shape[0]
    segment = departure_cells.shape[1] // lon_count
    var_dev = variables // lon_count
    columns = band_count * slot_dev
    slot_rows = lon_count * columns
    my_slots = (lax.axis_index("band") * lon_count + lon_index) * slot_dev + jnp.arange(
        slot_dev, dtype=jnp.int32
    )
    pair_ids = jnp.take(slot_pair, my_slots)
    fourier = inverse_legendre(spectral_in, leg_synthesis, pair_ids)
    outgoing = fourier.reshape(1, slot_dev, 2, 2, variables, fourier.shape[3])
    arrived = lax.all_to_all(
        lax.all_to_all(outgoing, "band", split_axis=5, concat_axis=1, tiled=True),
        "lon",
        split_axis=4,
        concat_axis=0,
        tiled=True,
    )
    spread = arrived.reshape(slot_rows * 4, var_dev * lat_band)
    wave_ids, active = slot_waves(
        slot_pair, jnp.arange(slot_rows, dtype=jnp.int32), lon_count, slot_dev
    )

    def synthesize(lon_block):
        longitudes = lon_block * segment + jnp.arange(segment, dtype=jnp.int32)
        basis = wave_basis(wave_ids, active, longitudes, True)
        return jnp.einsum("et,ec->tc", basis, spread, precision=lax.Precision.HIGHEST)

    circle = lax.map(synthesize, jnp.arange(lon_count, dtype=jnp.int32))
    local_grid = lax.all_to_all(circle, "lon", split_axis=0, concat_axis=2, tiled=True).reshape(
        segment, variables * lat_band
    )
    west_edge = from_behind(local_grid[segment - REACH :], "lon", 1)
    extended = jnp.concatenate([west_edge, local_grid], axis=0)
    shift_cells = lax.dynamic_slice_in_dim(departure_cells, lon_index * segment, segment, 1).T
    fraction = lax.dynamic_slice_in_dim(departure_frac, lon_index * segment, segment, 1).T
    advected = jnp.zeros_like(local_grid)
    for offset in range(REACH + 1):
        weight = jnp.where(shift_cells == offset, 1.0 - fraction, 0.0) + jnp.where(
            shift_cells == offset - 1, fraction, 0.0
        )
        advected = (
            advected
            + jnp.tile(weight, (1, variables)) * extended[REACH - offset : REACH - offset + segment]
        )
    returning = advected.reshape(segment, lon_count, var_dev * lat_band)
    field_rows = lax.all_to_all(returning, "lon", split_axis=1, concat_axis=0, tiled=True).reshape(
        lon_count * segment, var_dev * lat_band
    )

    def analyse(running, lon_block):
        longitudes = lon_block * segment + jnp.arange(segment, dtype=jnp.int32)
        basis = wave_basis(wave_ids, active, longitudes, False)
        block_rows = lax.dynamic_slice_in_dim(field_rows, lon_block * segment, segment, 0)
        return (
            running + jnp.einsum("et,tc->ec", basis, block_rows, precision=lax.Precision.HIGHEST),
            None,
        )

    starting = jnp.zeros((wave_ids.size * 2, var_dev * lat_band), jnp.float32)
    coefficients, unused = lax.scan(analyse, starting, jnp.arange(lon_count, dtype=jnp.int32))
    leaving = coefficients.reshape(lon_count, columns, 2, 2, var_dev * lat_band)
    returned = lax.all_to_all(
        lax.all_to_all(leaving, "band", split_axis=1, concat_axis=4, tiled=True),
        "lon",
        split_axis=0,
        concat_axis=4,
        tiled=True,
    )
    ordered = returned.reshape(slot_dev, 2, 2, lon_count, band_count, var_dev, lat_band)
    ordered = jnp.transpose(ordered, (0, 1, 2, 3, 5, 4, 6))
    analysis = ordered.reshape(slot_dev, 2, doubled, band_count * lat_band)
    return direct_legendre(analysis, leg_analysis, pair_ids)


def solution(mesh):
    return jax.shard_map(
        per_device,
        mesh=mesh,
        in_specs=(
            P(("band", "lon"), None, None),
            P(("band", "lon"), None, None),
            P(("band", "lon"), None, None),
            P(),
            P("band", None),
            P("band", None),
        ),
        out_specs=P(("band", "lon"), None, None),
        check_vma=False,
    )
```

profile of v0, /device:TPU:1, one launch (start us, length us, event | category | flops | bytes accessed | tf_op | source)
XLA Modules:
  0.0 541.8 jit_solution(2121400872011203226)
XLA Ops:
  11.1 14.8 %all-to-all-start = ((f32[64,1,1280]{2,1,0:T(1,128)}), f32[64,1,1280]{2,1,0:T(1,128)S(1)}, u32[]{:S(2)}, u32[]{:S(2)}) async-start(f32[64,1,1280]{2,1,0:T(1,128)} %reshape.513), calls=%async_computation | async-start | bytes 655360 | tf_op jit(solution)/shard_map/all_to_all | solution.py:112
  26.0 14.2 %all-to-all-done = f32[64,1,1280]{2,1,0:T(1,128)S(1)} async-done(((f32[64,1,1280]{2,1,0:T(1,128)}), f32[64,1,1280]{2,1,0:T(1,128)S(1)}, u32[]{:S(2)}, u32[]{:S(2)}) %all-to-all-start) | async-done | bytes 327712 | tf_op jit(solution)/shard_map/all_to_all | solution.py:112
  53.1 7.0 %all-to-all-start.1 = ((f32[8,1,10240]{2,1,0:T(1,128)}), f32[8,1,10240]{2,1,0:T(1,128)S(1)}, u32[]{:S(2)}, u32[]{:S(2)}) async-start(f32[8,1,10240]{2,1,0:T(1,128)} %reshape.515), calls=%async_computation.1 | async-start | bytes 655360 | tf_op jit(solution)/shard_map/all_to_all | solution.py:111
  63.7 10.1 %all-to-all-done.1 = f32[8,1,10240]{2,1,0:T(1,128)S(1)} async-done(((f32[8,1,10240]{2,1,0:T(1,128)}), f32[8,1,10240]{2,1,0:T(1,128)S(1)}, u32[]{:S(2)}, u32[]{:S(2)}) %all-to-all-start.1) | async-done | bytes 327712 | tf_op jit(solution)/shard_map/all_to_all | solution.py:111
  79.7 175.7 %while.26 = (s32[]{:T(128)}, f32[8,320,40]{1,2,0:T(8,128)}, s32[512,2]{0,1:T(2,128)S(1)}, s32[8]{0:T(128)S(1)}, f32[512,1]{0,1:T(1,128)S(1)}, /*index=5*/f32[2048,40]{1,0:T(8,128)}, s32[]{:T(128)}, s32[1]{0:T(128)}) while((s32[]{:T(128)}, f32[8,320,40]{1,2,0:T(8,128)}, s32[512,2]{0,1:T(2,128)S(1)}, s32[8]{0:T(128)S(1)}, ...), condition=%wide.region_1.2_spmd, body=%wide.region_0.1_spmd.sunk | while | flops 319163712 | bytes 22144112 | solution.py:128
  81.0 5.4 fusion.86
  102.9 5.4 fusion.86
  124.9 5.4 fusion.86
  146.9 5.4 fusion.86
  168.9 5.4 fusion.86
  190.8 5.4 fusion.86
  212.8 5.4 fusion.86
  234.7 5.4 fusion.86
  259.9 16.2 %all-to-all-done.2 = f32[8,320,40]{1,2,0:T(8,128)S(1)} async-done(((f32[8,320,40]{1,2,0:T(8,128)}), f32[8,320,40]{1,2,0:T(8,128)S(1)}, u32[]{:S(2)}, u32[]{:S(2)}) %all-to-all-start.2) | async-done | bytes 409632 | tf_op jit(solution)/shard_map/all_to_all | solution.py:129
  291.8 15.8 %all-to-all-done.3 = f32[320,8,40]{0,2,1:T(8,128)S(1)} async-done(((f32[320,8,40]{0,2,1:T(8,128)}), f32[320,8,40]{0,2,1:T(8,128)S(1)}, u32[]{:S(2)}, u32[]{:S(2)}) %all-to-all-start.3) | async-done | bytes 409632 | tf_op jit(solution)/shard_map/all_to_all | solution.py:146
  309.0 174.4 %while.27 = (s32[]{:T(128)}, f32[2048,40]{0,1:T(8,128)S(1)}, s32[512,2]{0,1:T(2,128)S(1)}, s32[8]{0:T(128)S(1)}, f32[512,1]{0,1:T(1,128)S(1)}, /*index=5*/f32[25...) while((s32[]{:T(128)}, f32[2048,40]{0,1:T(8,128)S(1)}, s32[512,2]{0,1:T(2,128)S(1)}, ...), condition=%wide.region_3.4_spmd.clone, body=%wide.region_2.3_spmd.clone.sunk | while | flops 319324992 | bytes 21836460 | solution.py:160
  310.2 5.4 fusion.91
  332.0 5.4 fusion.91
  353.7 5.4 fusion.91
  375.5 5.4 fusion.91
  397.2 5.4 fusion.91
  419.0 5.4 fusion.91
  486.5 20.0 %all_to_all.96 = f32[64,1,1280]{2,1,0:T(1,128)S(1)} all-to-all(f32[64,1,1280]{2,1,0:T(1,128)S(1)} %reshape.517), channel_id=1, replica_groups=mesh['band'=64,'lon'=8] {'band'}, dimensions={0} | all-to-all | bytes 655360 | tf_op jit(solution)/shard_map/all_to_all | solution.py:163
  516.0 13.6 %all-to-all-done.5 = f32[8,1,2,2,2560]{4,3,2,1,0:T(2,128)S(1)} async-done(((f32[8,1,2,2,2560]{4,3,2,1,0:T(2,128)}), f32[8,1,2,2,2560]{4,3,2,1,0:T(2,128)S(1)}, u32[]{:S(2)}, u32[]{:S(2)}) %all-to-all-start.5) | async-done | bytes 327712 | tf_op jit(solution)/shard_map/all_to_all | solution.py:162
  (230 shorter events, 342.7 us)
Async XLA Ops:
  11.1 29.0 %all-to-all-start = ((f32[64,1,1280]{2,1,0:T(1,128)}), f32[64,1,1280]{2,1,0:T(1,128)S(1)}, u32[]{:S(2)}, u32[]{:S(2)}) async-start(f32[64,1,1280]{2,1,0:T(1,128)} %reshape.513), calls=%async_computation | async-start | bytes 655360 | tf_op jit(solution)/shard_map/all_to_all | solution.py:112
  51.7 8.5 %copy-start = (s32[512]{0:T(512)S(1)}, s32[512]{0:T(512)}, u32[]{:S(2)}) copy-start(s32[512]{0:T(512)} %param.13) | copy-start | bytes 6148
  53.1 20.7 %all-to-all-start.1 = ((f32[8,1,10240]{2,1,0:T(1,128)}), f32[8,1,10240]{2,1,0:T(1,128)S(1)}, u32[]{:S(2)}, u32[]{:S(2)}) async-start(f32[8,1,10240]{2,1,0:T(1,128)} %reshape.515), calls=%async_computation.1 | async-start | bytes 655360 | tf_op jit(solution)/shard_map/all_to_all | solution.py:111
  255.4 20.7 %all-to-all-start.2 = ((f32[8,320,40]{1,2,0:T(8,128)}), f32[8,320,40]{1,2,0:T(8,128)S(1)}, u32[]{:S(2)}, u32[]{:S(2)}) async-start(f32[8,320,40]{1,2,0:T(8,128)} %get-tuple-element.161), calls=%async_computation.2 | async-start | bytes 983040 | tf_op jit(solution)/shard_map/all_to_all | solution.py:129
  276.9 8.7 %collective-permute-start = (f32[4,320]{0,1:T(8,128)}, f32[4,320]{0,1:T(8,128)}, u32[]{:S(2)}, u32[]{:S(2)}) collective-permute-start(f32[4,320]{0,1:T(8,128)} %bitcast.26), channel_id=1, source_target_pairs={{0,1},{1,2},{2,3},{3,4},{4,5},{5,6},{6,7},{7,0},{8,9},{9,10},{10,1... | collective-permute-start | bytes 15368 | tf_op jit(solution)/shard_map/ppermute | solution.py:18
  288.3 19.3 %all-to-all-start.3 = ((f32[320,8,40]{0,2,1:T(8,128)}), f32[320,8,40]{0,2,1:T(8,128)S(1)}, u32[]{:S(2)}, u32[]{:S(2)}) async-start(f32[320,8,40]{0,2,1:T(8,128)} %bitcast.31), calls=%async_computation.3 | async-start | bytes 983040 | tf_op jit(solution)/shard_map/all_to_all | solution.py:146
  512.3 17.3 %all-to-all-start.5 = ((f32[8,1,2,2,2560]{4,3,2,1,0:T(2,128)}), f32[8,1,2,2,2560]{4,3,2,1,0:T(2,128)S(1)}, u32[]{:S(2)}, u32[]{:S(2)}) async-start(f32[8,1,2,2,2560]{4,3,2,1,0:T(2,128)} %reshape.511), calls=%async_computation.5 | async-start | bytes 655360 | tf_op jit(solution)/shard_map/all_to_all | solution.py:162
  537.9 1.4 copy-start.1
where the time goes:
time: 553 us; the launch traced here: 542 us
  local copies, waits for them, and re-layouts  226 us (41%)
  other arithmetic  98.9 us (18%)
  matrix products  75.2 us (14%)
  waiting for transfers between devices  75 us (14%)
  starting transfers between devices  34.5 us (6%)
  blocking collectives  20 us (4%)
  loops' own time  10.9 us (2%)
    another operation x32, local copies, waits for them, and re-layouts, wave_basis(): jnp.stack([jnp.cos(angles), -jnp.sin(angles)], axis=-2)  120 us
    cos x16, other arithmetic, wave_basis(): jnp.cos(angles)  85.8 us
    mul x32, local copies, waits for them, and re-layouts, wave_basis(): jnp.stack([jnp.cos(angles), -jnp.sin(angles)], axis=-2)  48.9 us
    dot_general x8, matrix products, analyse(): jnp.einsum('et,tc->ec', basis, block_rows, precision=lax.Precision.HIGHEST)  35.2 us
    dot_general x8, matrix products, synthesize(): jnp.einsum('et,ec->tc', basis, spread, precision=lax.Precision.HIGHEST)  35 us
    all_to_all x1, blocking collectives, per_device(): lax.all_to_all(leaving, 'band', split_axis=1, concat_axis=4, tiled=True)  20 us
    all_to_all x1, waiting for transfers between devices, per_device(): lax.all_to_all(circle, 'lon', split_axis=0, concat_axis=2, tiled=True)  16.2 us
    unnamed x11, local copies, waits for them, and re-layouts  15.8 us
  transfers between devices with their start and end apart: 6, of which 6 were waited for; matrix products, arithmetic and copies ran while one was open for 1% of the time, Pallas kernels for 0%

commit v1 on v0

v1 whole, which is shorter than its diff:
```python
import math

import jax
import jax.numpy as jnp
import ml_dtypes
import numpy as np
from jax import lax
from jax.experimental import pallas as pl
from jax.experimental.pallas import tpu as pltpu
from jax.sharding import PartitionSpec as P

WAVES = 640
PAIRS = 320
ROWS = 641
HALF = 640
NLON = 2560
SLOTS = 512
RADIX = 8
FINE = 80
SEG = 320
WIDE = 384
HALF_ROWS = 5
REACH = 4
BF = jnp.bfloat16
F32 = jnp.float32


def halves(table):
    high = table.astype(np.float32).astype(ml_dtypes.bfloat16)
    low = (table - high.astype(np.float64)).astype(np.float32).astype(ml_dtypes.bfloat16)
    return high, low


def fine_tables():
    place = np.arange(WIDE)
    place = np.where(place < SEG, place, place - WIDE)
    phase = (np.arange(FINE)[:, None] * place[None, :]) % SEG
    cos, sin = np.cos(2 * math.pi * phase / SEG), np.sin(2 * math.pi * phase / SEG)
    synth = np.zeros((256, 2 * WIDE))
    synth[0:FINE, :WIDE] = 2 * cos
    synth[0:FINE, WIDE:] = 2 * sin
    synth[128 : 128 + FINE, :WIDE] = -2 * sin
    synth[128 : 128 + FINE, WIDE:] = 2 * cos
    anal = np.zeros((2 * WIDE, 256))
    anal[:WIDE, 0:FINE] = cos.T / NLON
    anal[WIDE:, 0:FINE] = sin.T / NLON
    anal[:WIDE, 128 : 128 + FINE] = -sin.T / NLON
    anal[WIDE:, 128 : 128 + FINE] = cos.T / NLON
    turn = 2 * math.pi * ((np.arange(RADIX)[:, None] * place[None, :]) % NLON) / NLON
    twiddle = np.concatenate([np.cos(turn), np.sin(turn)], axis=0).astype(np.float32)
    return halves(synth), halves(anal), twiddle


def split(value):
    high = value.astype(BF)
    return high, (value - high.astype(F32)).astype(BF)


def dot3(left, right_high, right_low):
    high, low = split(left)
    rows = left.shape[0]
    both = jnp.dot(
        jnp.concatenate([high, low], axis=0), right_high, preferred_element_type=F32
    )
    return both[:rows] + both[rows:] + jnp.dot(high, right_low, preferred_element_type=F32)


def wave_rows(pair):
    row = lax.broadcasted_iota(jnp.int32, (1, ROWS), 1)
    cut = WAVES - pair
    upper = row < cut
    odd = jnp.where(upper, row, row - cut) & 1
    return upper, odd


def synthesis_kernel(slot_ref, pairs_ref, spec_ref, table_ref, out_ref, turned, staged):
    pair = pairs_ref[slot_ref[0]]
    upper, odd = wave_rows(pair)
    live = pair < PAIRS
    groups = []
    for parity in range(2):
        for half in range(2):
            for wave in range(2):
                mask = jnp.logical_and(upper if wave == 0 else jnp.logical_not(upper), odd == parity)
                mask = jnp.logical_and(mask, live)
                for part in range(2):
                    first = part * 16 + half * 8
                    groups.append(jnp.where(mask, spec_ref[0, first : first + 8, :], 0.0))
    table_high, table_low = split(table_ref[0])
    product = dot3(jnp.concatenate(groups, axis=0), table_high, table_low)
    even, odd_sum = product[:64], product[64:]
    turned[...] = jnp.concatenate([even + odd_sum, even - odd_sum], axis=0).T
    lane = lax.broadcasted_iota(jnp.int32, (128, 128), 1)
    left = lane < 64
    pick = [turned[pl.ds(u, 128, stride=5), :] for u in range(5)]
    rolled = [pltpu.roll(q, 64, 1) for q in pick]
    staged[pl.ds(0, 128, stride=2), :] = jnp.where(left, pick[0], rolled[1])
    staged[pl.ds(1, 128, stride=2), :] = jnp.where(left, pick[3], rolled[4])
    staged[pl.ds(256, 128, stride=2), :] = pick[2]
    staged[pl.ds(257, 128, stride=2), :] = pltpu.roll(pick[2], 96, 1)
    staged[pl.ds(512, 128, stride=2), :] = jnp.where(left, rolled[0], pick[1])
    staged[pl.ds(513, 128, stride=2), :] = jnp.where(left, rolled[3], pick[4])
    staged[pl.ds(768, 128, stride=2), :] = rolled[2]
    staged[pl.ds(769, 128, stride=2), :] = pltpu.roll(pick[2], 32, 1)
    out_ref[0:256, 0:128] = staged[0:256, :]
    out_ref[0:256, 128:256] = staged[256:512, :]
    for block in range(32):
        at = (63 - block) * 8
        out_ref[at : at + 8, 0:128] = staged[512 + block * 8 : 512 + block * 8 + 8, :]
        out_ref[at : at + 8, 128:256] = staged[768 + block * 8 : 768 + block * 8 + 8, :]


def grid_kernel(
    in_ref, choice_ref, weight_ref, synth_h, synth_l, anal_h, anal_l, twiddle_ref, out_ref,
    coeff, spread, fields, back
):
    columns = in_ref[...].T[:160]
    high, low = split(columns)
    picked = jnp.dot(
        jnp.concatenate([high, low], axis=0), choice_ref[...], preferred_element_type=F32
    )
    lane = lax.broadcasted_iota(jnp.int32, (8, 128), 1)
    first_wave = lane < FINE // 2
    mean_scale = jnp.where(lane == 0, 0.5, 1.0)
    for level in range(2):
        for i in range(HALF_ROWS):
            for r in range(RADIX):
                for part in range(2):
                    base = level * 160 + i * 32 + part * 8
                    value = jnp.where(
                        first_wave,
                        picked[base : base + 8, r * 128 : r * 128 + 128],
                        picked[base + 16 : base + 24, r * 128 : r * 128 + 128],
                    )
                    if r == 0:
                        value = value * mean_scale
                    at = level * 320 + i * 64 + r * 8
                    coeff[at : at + 8, part * 128 : part * 128 + 128] = value
    both = coeff[...].astype(BF)
    wide = jnp.dot(both, synth_h[...], preferred_element_type=F32)
    spread[...] = (
        wide[:320] + wide[320:] + jnp.dot(both[:320], synth_l[...], preferred_element_type=F32)
    )
    root = math.sqrt(0.5)
    for i in range(HALF_ROWS):
        real, imag = [], []
        for r in range(RADIX):
            at = i * 64 + r * 8
            zr, zi = spread[at : at + 8, :WIDE], spread[at : at + 8, WIDE:]
            if r == 0:
                real.append(zr)
                imag.append(None)
                continue
            tr, ti = twiddle_ref[r : r + 1, :], twiddle_ref[RADIX + r : RADIX + r + 1, :]
            real.append(tr * zr - ti * zi)
            imag.append(None if r == 4 else tr * zi + ti * zr)
        plus, minus = real[0] + real[4], real[0] - real[4]
        p, n = real[2] + real[6], imag[2] - imag[6]
        evens = [plus + p, minus - n, plus - p, minus + n]
        a, b = real[1] + real[7], real[3] + real[5]
        c, d = imag[1] - imag[7], imag[3] - imag[5]
        odds = [a + b, root * ((a - b) - (c + d)), d - c, -root * ((a - b) + (c + d))]
        moved = []
        for k in range(RADIX):
            value = evens[k] + odds[k] if k < 4 else evens[k - 4] - odds[k - 4]
            total = weight_ref[i, k, 0:1, :] * value
            for offset in range(1, REACH + 1):
                total = total + weight_ref[i, k, offset : offset + 1, :] * pltpu.roll(
                    value, offset, 1
                )
            moved.append(total)
        s = [moved[k] + moved[k + 4] for k in range(4)]
        d = [moved[k] - moved[k + 4] for k in range(4)]
        s02, s13 = s[0] + s[2], s[1] + s[3]
        dd, ds = root * (d[1] - d[3]), root * (d[1] + d[3])
        waves = [
            (s02 + s13, None),
            (d[0] + dd, -d[2] - ds),
            (s[0] - s[2], s[3] - s[1]),
            (d[0] - dd, d[2] - ds),
            (s02 - s13, None),
        ]
        for r in range(RADIX):
            vr, vi = waves[r] if r < 5 else waves[8 - r]
            if r > 4:
                vi = -vi
            at = i * 64 + r * 8
            if r == 0:
                fields[at : at + 8, :WIDE] = vr
                fields[at : at + 8, WIDE:] = jnp.zeros_like(vr)
                continue
            tr, ti = twiddle_ref[r : r + 1, :], twiddle_ref[RADIX + r : RADIX + r + 1, :]
            if vi is None:
                fields[at : at + 8, :WIDE] = tr * vr
                fields[at : at + 8, WIDE:] = -ti * vr
            else:
                fields[at : at + 8, :WIDE] = tr * vr + ti * vi
                fields[at : at + 8, WIDE:] = tr * vi - ti * vr
    result = dot3(fields[...], anal_h[...], anal_l[...])
    for i in range(HALF_ROWS):
        for r in range(RADIX):
            for part in range(2):
                at = i * 64 + r * 8
                value = result[at : at + 8, part * 128 : part * 128 + 128]
                base = i * 32 + part * 8
                back[base : base + 8, r * 128 : r * 128 + 128] = jnp.where(first_wave, value, 0.0)
                back[base + 16 : base + 24, r * 128 : r * 128 + 128] = jnp.where(
                    first_wave, 0.0, value
                )
    high, low = split(back[...])
    across = (((1,), (1,)), ((), ()))
    choice = choice_ref[...]
    out_ref[:, 0:160] = lax.dot_general(
        choice, high, across, preferred_element_type=F32
    ) + lax.dot_general(choice, low, across, preferred_element_type=F32)
    out_ref[:, 160:256] = jnp.zeros((SLOTS, 96), F32)


def analysis_kernel(slot_ref, pairs_ref, in_ref, table_ref, out_ref, turned, staged):
    staged[0:256, :] = in_ref[0:256, 0:128]
    staged[256:512, :] = in_ref[0:256, 128:256]
    for block in range(32):
        at = (63 - block) * 8
        staged[512 + block * 8 : 512 + block * 8 + 8, :] = in_ref[at : at + 8, 0:128]
        staged[768 + block * 8 : 768 + block * 8 + 8, :] = in_ref[at : at + 8, 128:256]
    lane = lax.broadcasted_iota(jnp.int32, (128, 128), 1)
    left = lane < 64
    north_a, north_b, south_a, south_b = (
        [staged[pl.ds(256 * q + f, 128, stride=2), :] for f in range(2)] for q in range(4)
    )
    for f in range(2):
        turned[pl.ds(3 * f, 128, stride=5), :] = jnp.where(
            left, north_a[f], pltpu.roll(south_a[f], 64, 1)
        )
        turned[pl.ds(3 * f + 1, 128, stride=5), :] = jnp.where(
            left, pltpu.roll(north_a[f], 64, 1), south_a[f]
        )
    turned[pl.ds(2, 128, stride=5), :] = jnp.where(
        left,
        jnp.where(lane < 32, north_b[0], pltpu.roll(north_b[1], 32, 1)),
        jnp.where(lane < 96, pltpu.roll(south_b[0], 64, 1), pltpu.roll(south_b[1], 96, 1)),
    )
    straight = turned[...].T
    north, south_rows = straight[:64], straight[64:]
    table_high, table_low = split(table_ref[0])
    product = dot3(
        jnp.concatenate([north + south_rows, north - south_rows], axis=0), table_high, table_low
    )
    pair = pairs_ref[slot_ref[0]]
    upper, odd = wave_rows(pair)
    live = pair < PAIRS
    even = odd == 0
    for half in range(2):
        for part in range(2):
            rows = [
                [
                    product[
                        parity * 64 + half * 32 + wave * 16 + part * 8 :
                        parity * 64 + half * 32 + wave * 16 + part * 8 + 8
                    ]
                    for parity in range(2)
                ]
                for wave in range(2)
            ]
            value = jnp.where(
                upper,
                jnp.where(even, rows[0][0], rows[0][1]),
                jnp.where(even, rows[1][0], rows[1][1]),
            )
            first = part * 16 + half * 8
            out_ref[0, first : first + 8, :] = jnp.where(live, value, 0.0)


SMEM = pl.BlockSpec(memory_space=pltpu.SMEM)
VMEM = pl.BlockSpec(memory_space=pltpu.VMEM)
PARAMS = pltpu.CompilerParams(vmem_limit_bytes=40 * 1024 * 1024)


def legendre_scratch():
    return [pltpu.VMEM((HALF, 128), F32), pltpu.VMEM((1024, 128), F32)]


def slot_choice(slot_pair):
    block = jnp.arange(RADIX * 128, dtype=jnp.int32)
    fine, rest = block % 128, block // 128
    wave = fine * RADIX + rest
    pair = jnp.where(wave < PAIRS, wave, WAVES - 1 - wave)
    pair = jnp.where(fine < FINE, pair, -1)
    return (slot_pair[:, None] == pair[None, :]).astype(BF)


def advection_weights(cells, fraction, band, lon, bands):
    position = jnp.arange(HALF_ROWS, dtype=jnp.int32)
    position = jnp.where(lon % 2 == 0, position, (position + 1) % HALF_ROWS)
    row = (HALF_ROWS * lon + position) // 2
    row = jnp.where(band < bands // 2, row, cells.shape[0] - 1 - row)
    cells = jnp.take(cells, row, axis=0).reshape(HALF_ROWS, RADIX, 1, SEG)
    fraction = jnp.take(fraction, row, axis=0).reshape(HALF_ROWS, RADIX, 1, SEG)
    offset = jnp.arange(REACH + 1, dtype=jnp.int32)[None, None, :, None]
    weight = jnp.where(cells == offset, 1.0 - fraction, 0.0) + jnp.where(
        cells == offset - 1, fraction, 0.0
    )
    return jnp.pad(weight, ((0, 0), (0, 0), (0, 0), (0, WIDE - SEG)))


def per_device(
    spectral_in, leg_synthesis, leg_analysis, slot_pair, departure_cells, departure_frac
):
    bands, lons = lax.axis_size("band"), lax.axis_size("lon")
    band, lon = lax.axis_index("band"), lax.axis_index("lon")
    slot = (band * lons + lon).astype(jnp.int32).reshape(1)
    outgoing = pl.pallas_call(
        synthesis_kernel,
        out_shape=jax.ShapeDtypeStruct((SLOTS, 256), F32),
        in_specs=[SMEM, SMEM, VMEM, VMEM],
        out_specs=VMEM,
        scratch_shapes=legendre_scratch(),
        compiler_params=PARAMS,
        name="legendre_synthesis",
    )(slot, slot_pair, spectral_in, leg_synthesis)
    arrived = lax.all_to_all(
        outgoing.reshape(SLOTS, 1, 256), ("band", "lon"), split_axis=0, concat_axis=0, tiled=True
    ).reshape(SLOTS, 256)
    choice = slot_choice(slot_pair)
    weights = advection_weights(departure_cells, departure_frac, band, lon, bands)
    (synth_h, synth_l), (anal_h, anal_l), twiddle = fine_tables()
    returning = pl.pallas_call(
        grid_kernel,
        out_shape=jax.ShapeDtypeStruct((SLOTS, 256), F32),
        in_specs=[VMEM] * 8,
        out_specs=VMEM,
        scratch_shapes=[
            pltpu.VMEM((640, 256), F32),
            pltpu.VMEM((320, 2 * WIDE), F32),
            pltpu.VMEM((320, 2 * WIDE), F32),
            pltpu.VMEM((160, 1024), F32),
        ],
        compiler_params=PARAMS,
        name="grid_step",
    )(arrived, choice, weights, synth_h, synth_l, anal_h, anal_l, twiddle)
    returned = lax.all_to_all(
        returning.reshape(SLOTS, 1, 256), ("band", "lon"), split_axis=0, concat_axis=0, tiled=True
    ).reshape(SLOTS, 256)
    return pl.pallas_call(
        analysis_kernel,
        out_shape=jax.ShapeDtypeStruct((1, 32, ROWS), F32),
        in_specs=[SMEM, SMEM, VMEM, VMEM],
        out_specs=VMEM,
        scratch_shapes=legendre_scratch(),
        compiler_params=PARAMS,
        name="legendre_analysis",
    )(slot, slot_pair, returned, leg_analysis)


def solution(mesh):
    return jax.shard_map(
        per_device,
        mesh=mesh,
        in_specs=(
            P(("band", "lon"), None, None),
            P(("band", "lon"), None, None),
            P(("band", "lon"), None, None),
            P(),
            P("band", None),
            P("band", None),
        ),
        out_specs=P(("band", "lon"), None, None),
        check_vma=False,
    )
```

time: 553 us -> 89.9 us (0.16); the launches traced: 542 us -> 89.5 us
  local copies, waits for them, and re-layouts: 226 us -> 10.2 us
  other arithmetic: 98.9 us -> 0.64 us
  matrix products: 75.2 us -> 0 us
  waiting for transfers between devices: 75 us -> 38 us
  blocking collectives: 20 us -> 0 us
  loops' own time: 10.9 us -> 0 us
  Pallas kernels: 0 us -> 7.72 us
    another operation x43 -> x0, local copies, waits for them, and re-layouts: 120 us -> none  [the longest x32 120 us: wave_basis(): jnp.stack([jnp.cos(angles), -jnp.sin(angles)], axis=-2)]
    cos x16 -> x0, other arithmetic: 85.8 us -> none  [wave_basis(): jnp.cos(angles)]
    dot_general x18 -> x0, matrix products: 75.2 us -> none  [the longest x8 35.2 us: analyse(): jnp.einsum('et,tc->ec', basis, block_rows, precision=lax.Precision.HIGHEST)]
    mul x40 -> x0, local copies, waits for them, and re-layouts: 50.1 us -> none  [the longest x32 48.9 us: wave_basis(): jnp.stack([jnp.cos(angles), -jnp.sin(angles)], axis=-2)]
    all_to_all x5 -> x2, waiting for transfers between devices: 69.9 us -> 38 us  [the longest x1 19.4 us: per_device(): lax.all_to_all(returning.reshape(SLOTS, 1, 256), ('band', 'lon'), split_a...]
    all_to_all x1 -> x0, blocking collectives: 20 us -> none  [per_device(): lax.all_to_all(leaving, 'band', split_axis=1, concat_axis=4, tiled=True)]
    all_to_all x9 -> x0, local copies, waits for them, and re-layouts: 11.2 us -> none  [the longest x3 6.6 us: per_device(): lax.all_to_all(outgoing, 'band', split_axis=5, concat_axis=1, tiled=True)]
    another operation x2 -> x0, loops' own time: 10.9 us -> none  [the longest x1 5.47 us: per_device(): lax.scan(analyse, starting, jnp.arange(lon_count, dtype=jnp.int32))]
  transfers between devices with their start and end apart: 6 -> 2, of which waited for: 6 -> 2; matrix products, arithmetic and copies ran while one was open for 1% -> 6% of each run, Pallas kernels for 0% -> 0%
where the time goes in v1:
time: 89.9 us; the launch traced here: 89.5 us
  waiting for transfers between devices  38 us (42%)
  starting transfers between devices  32.7 us (36%)
  local copies, waits for them, and re-layouts  10.2 us (11%)
  Pallas kernels  7.72 us (9%)
    all_to_all x1, starting transfers between devices, per_device(): lax.all_to_all(outgoing.reshape(SLOTS, 1, 256), ('band', 'lon'), split_ax...  24.2 us
    all_to_all x1, waiting for transfers between devices, per_device(): lax.all_to_all(returning.reshape(SLOTS, 1, 256), ('band', 'lon'), split_a...  19.4 us
    all_to_all x1, waiting for transfers between devices, per_device(): lax.all_to_all(outgoing.reshape(SLOTS, 1, 256), ('band', 'lon'), split_ax...  18.6 us
    all_to_all x1, starting transfers between devices, per_device(): lax.all_to_all(returning.reshape(SLOTS, 1, 256), ('band', 'lon'), split_a...  8.44 us
    unnamed x22, local copies, waits for them, and re-layouts  6.2 us
    pallas_call x1, Pallas kernels, per_device(): pl.pallas_call(grid_kernel, out_shape=jax.ShapeDtypeStruct((SLOTS, 256),...  3.9 us
    pallas_call x1, Pallas kernels, per_device(): pl.pallas_call(analysis_kernel, out_shape=jax.ShapeDtypeStruct((1, 32, RO...  2.28 us
  transfers between devices with their start and end apart: 2, of which 2 were waited for; matrix products, arithmetic and copies ran while one was open for 6% of the time, Pallas kernels for 0%

profile of v1, /device:TPU:1, one launch (start us, length us, event | category | flops | bytes accessed | tf_op | source)
XLA Modules:
  0.0 89.5 jit_solution(3183780483448115160)
XLA Ops:
  0.0 1.6 %copy.14.table_ref = f32[1,641,640]{2,1,0:T(8,128)S(1)} copy(f32[1,641,640]{2,0,1:T(1,128)} %param.12) | data formatting | bytes 3281920 | tf_op args[1]
  1.6 1.5 %legendre_synthesis.1 = f32[512,256]{1,0:T(8,128)S(1)} custom-call(s32[1]{0:T(128)} %bitcast.slot_ref, s32[512]{0:T(512)S(1)} %copy-done.7, f32[1,32,641]{2,1,0:T(8,128)S(1)} %copy-done.5, f32[1,641,640]{2,1,0:T(8,128)S(1)} %copy.14.table_ref), custom_call_target="tpu_custom_call" | custom-call | tf_op jit(solution)/shard_map/legendre_synthesis/pallas_call | solution.py:312
  3.2 0.0 copy-start.8
  3.2 1.3 %copy.15 = f32[512,1,256]{2,1,0:T(1,128)} copy(f32[512,1,256]{2,0,1:T(8,128)S(1)} %bitcast.12) | data formatting | bytes 1048576 | tf_op jit(solution)/shard_map/reshape | solution.py:322
  4.5 24.2 %all-to-all-start = ((f32[512,1,256]{2,1,0:T(1,128)}), f32[512,1,256]{2,1,0:T(1,128)}, u32[]{:S(2)}, u32[]{:S(2)}) async-start(f32[512,1,256]{2,1,0:T(1,128)} %copy.15), calls=%async_computation | async-start | bytes 1048576 | tf_op jit(solution)/shard_map/all_to_all | solution.py:321
  28.9 0.6 gather_fusion.1
  29.4 0.1 gather.15
  29.5 0.6 gather_fusion
  30.1 0.1 gather.13
  30.2 0.1 broadcast_select_fusion.1
  30.3 0.0 copy-start.3
  30.3 0.0 copy-start.4
  30.3 0.0 copy-start.6
  30.3 0.1 broadcast_subtract_fusion
  30.4 0.2 select_add_fusion
  30.6 0.2 compare_convert_fusion.choice_ref
  30.9 18.6 %all-to-all-done = f32[512,1,256]{2,1,0:T(1,128)} async-done(((f32[512,1,256]{2,1,0:T(1,128)}), f32[512,1,256]{2,1,0:T(1,128)}, u32[]{:S(2)}, u32[]{:S(2)}) %all-to-all-start) | async-done | bytes 524320 | tf_op jit(solution)/shard_map/all_to_all | solution.py:321
  49.5 1.1 %copy.23 = f32[512,1,256]{2,0,1:T(8,128)S(1)} copy(f32[512,1,256]{2,1,0:T(1,128)} %all-to-all-done) | data formatting | bytes 1048576
  50.7 3.9 %grid_step.1 = f32[512,256]{1,0:T(8,128)S(1)} custom-call(f32[512,256]{1,0:T(8,128)S(1)} %bitcast.13, bf16[512,1024]{1,0:T(8,128)(2,1)S(1)} %compare_convert_fusion.choice_ref, f32[5,8,5,384]{3,2,1,0:T(8,128)S(1)} %pad.4.weight_ref, bf16[256,768]{1,0:T(8,128)(2,1)S(1)} %copy-done.1, bf16[256,768]{1,0:T(8,128)(2,1)S(1)} %copy-done.2, ...), custom_call_target="tpu_custom_call" | custom-call | tf_op jit(solution)/shard_map/grid_step/pallas_call | solution.py:327
  54.6 1.3 %copy.16 = f32[512,1,256]{2,1,0:T(1,128)} copy(f32[512,1,256]{2,0,1:T(8,128)S(1)} %bitcast.14) | data formatting | bytes 1048576 | tf_op jit(solution)/shard_map/reshape | solution.py:342
  55.9 8.4 %all-to-all-start.1 = ((f32[512,1,256]{2,1,0:T(1,128)}), f32[512,1,256]{2,1,0:T(1,128)S(1)}, u32[]{:S(2)}, u32[]{:S(2)}) async-start(f32[512,1,256]{2,1,0:T(1,128)} %copy.16), calls=%async_computation.1 | async-start | bytes 1048576 | tf_op jit(solution)/shard_map/all_to_all | solution.py:341
  64.4 3.5 %copy.17.table_ref = f32[1,640,641]{2,1,0:T(8,128)S(1)} copy(f32[1,640,641]{1,0,2:T(1,128)} %param.13) | data formatting | bytes 3281920 | tf_op args[2]
  67.8 19.4 %all-to-all-done.1 = f32[512,1,256]{2,1,0:T(1,128)S(1)} async-done(((f32[512,1,256]{2,1,0:T(1,128)}), f32[512,1,256]{2,1,0:T(1,128)S(1)}, u32[]{:S(2)}, u32[]{:S(2)}) %all-to-all-start.1) | async-done | bytes 524320 | tf_op jit(solution)/shard_map/all_to_all | solution.py:341
  87.2 2.3 %legendre_analysis.1 = f32[1,32,641]{2,1,0:T(8,128)} custom-call(s32[1]{0:T(128)} %bitcast.slot_ref, s32[512]{0:T(512)S(1)} %copy-done.7, f32[512,256]{1,0:T(8,128)S(1)} %bitcast.11, f32[1,640,641]{2,1,0:T(8,128)S(1)} %copy.17.table_ref), custom_call_target="tpu_custom_call" | custom-call | tf_op jit(solution)/shard_map/legendre_analysis/pallas_call | solution.py:344
  (21 shorter events, 0.2 us)
Async XLA Ops:
  0.0 28.9 %copy-start = (f32[20,2560]{1,0:T(8,128)S(1)}, f32[20,2560]{1,0:T(8,128)}, u32[]{:S(2)}) copy-start(f32[20,2560]{1,0:T(8,128)} %param.16) | copy-start | bytes 614404
  0.0 1.6 %copy-start.7 = (s32[512]{0:T(512)S(1)}, s32[512]{0:T(512)}, u32[]{:S(2)}) copy-start(s32[512]{0:T(512)} %pairs_ref.3) | copy-start | bytes 6148
  0.0 1.6 %copy-start.5 = (f32[1,32,641]{2,1,0:T(8,128)S(1)}, f32[1,32,641]{2,1,0:T(8,128)}, u32[]{:S(2)}) copy-start(f32[1,32,641]{2,1,0:T(8,128)} %spec_ref.1) | copy-start | bytes 246148
  3.2 26.4 %copy-start.8 = (s32[20,2560]{1,0:T(8,128)S(1)}, s32[20,2560]{1,0:T(8,128)}, u32[]{:S(2)}) copy-start(s32[20,2560]{1,0:T(8,128)} %param.15) | copy-start | bytes 614404
  4.5 45.0 %all-to-all-start = ((f32[512,1,256]{2,1,0:T(1,128)}), f32[512,1,256]{2,1,0:T(1,128)}, u32[]{:S(2)}, u32[]{:S(2)}) async-start(f32[512,1,256]{2,1,0:T(1,128)} %copy.15), calls=%async_computation | async-start | bytes 1048576 | tf_op jit(solution)/shard_map/all_to_all | solution.py:321
  30.3 20.3 %copy-start.1 = (bf16[256,768]{1,0:T(8,128)(2,1)S(1)}, bf16[256,768]{1,0:T(8,128)(2,1)}, u32[]{:S(2)}) copy-start(bf16[256,768]{1,0:T(8,128)(2,1)} %constant.132.clone.synth_h) | copy-start | bytes 1179652
  30.3 20.3 %copy-start.2 = (bf16[256,768]{1,0:T(8,128)(2,1)S(1)}, bf16[256,768]{1,0:T(8,128)(2,1)}, u32[]{:S(2)}) copy-start(bf16[256,768]{1,0:T(8,128)(2,1)} %constant.133.clone.synth_l) | copy-start | bytes 1179652
  30.3 20.3 %copy-start.3 = (bf16[768,256]{1,0:T(8,128)(2,1)S(1)}, bf16[768,256]{1,0:T(8,128)(2,1)}, u32[]{:S(2)}) copy-start(bf16[768,256]{1,0:T(8,128)(2,1)} %constant.134.clone.anal_h) | copy-start | bytes 1179652
  30.3 20.3 %copy-start.4 = (bf16[768,256]{1,0:T(8,128)(2,1)S(1)}, bf16[768,256]{1,0:T(8,128)(2,1)}, u32[]{:S(2)}) copy-start(bf16[768,256]{1,0:T(8,128)(2,1)} %constant.135.clone.anal_l) | copy-start | bytes 1179652
  30.3 20.3 %copy-start.6 = (f32[16,384]{1,0:T(8,128)S(1)}, f32[16,384]{1,0:T(8,128)}, u32[]{:S(2)}) copy-start(f32[16,384]{1,0:T(8,128)} %constant.136.clone.twiddle_ref) | copy-start | bytes 73732
  55.9 31.3 %all-to-all-start.1 = ((f32[512,1,256]{2,1,0:T(1,128)}), f32[512,1,256]{2,1,0:T(1,128)S(1)}, u32[]{:S(2)}, u32[]{:S(2)}) async-start(f32[512,1,256]{2,1,0:T(1,128)} %copy.16), calls=%async_computation.1 | async-start | bytes 1048576 | tf_op jit(solution)/shard_map/all_to_all | solution.py:341

commit v2 on v1

--- a/solution.py
+++ b/solution.py
@@ -73,7 +73,7 @@
     return upper, odd
 
 
-def synthesis_kernel(slot_ref, pairs_ref, spec_ref, table_ref, out_ref, turned, staged):
+def synthesis_kernel(slot_ref, pairs_ref, spec_ref, table_ref, out_ref, turned, south):
     pair = pairs_ref[slot_ref[0]]
     upper, odd = wave_rows(pair)
     live = pair < PAIRS
@@ -94,27 +94,26 @@
     left = lane < 64
     pick = [turned[pl.ds(u, 128, stride=5), :] for u in range(5)]
     rolled = [pltpu.roll(q, 64, 1) for q in pick]
-    staged[pl.ds(0, 128, stride=2), :] = jnp.where(left, pick[0], rolled[1])
-    staged[pl.ds(1, 128, stride=2), :] = jnp.where(left, pick[3], rolled[4])
-    staged[pl.ds(256, 128, stride=2), :] = pick[2]
-    staged[pl.ds(257, 128, stride=2), :] = pltpu.roll(pick[2], 96, 1)
-    staged[pl.ds(512, 128, stride=2), :] = jnp.where(left, rolled[0], pick[1])
-    staged[pl.ds(513, 128, stride=2), :] = jnp.where(left, rolled[3], pick[4])
-    staged[pl.ds(768, 128, stride=2), :] = rolled[2]
-    staged[pl.ds(769, 128, stride=2), :] = pltpu.roll(pick[2], 32, 1)
-    out_ref[0:256, 0:128] = staged[0:256, :]
-    out_ref[0:256, 128:256] = staged[256:512, :]
+    out_ref[pl.ds(0, 128, stride=4), :] = jnp.where(left, pick[0], rolled[1])
+    out_ref[pl.ds(1, 128, stride=4), :] = pick[2]
+    out_ref[pl.ds(2, 128, stride=4), :] = jnp.where(left, pick[3], rolled[4])
+    out_ref[pl.ds(3, 128, stride=4), :] = pltpu.roll(pick[2], 96, 1)
+    south[pl.ds(0, 128, stride=4), :] = jnp.where(left, rolled[0], pick[1])
+    south[pl.ds(1, 128, stride=4), :] = rolled[2]
+    south[pl.ds(2, 128, stride=4), :] = jnp.where(left, rolled[3], pick[4])
+    south[pl.ds(3, 128, stride=4), :] = pltpu.roll(pick[2], 32, 1)
     for block in range(32):
-        at = (63 - block) * 8
-        out_ref[at : at + 8, 0:128] = staged[512 + block * 8 : 512 + block * 8 + 8, :]
-        out_ref[at : at + 8, 128:256] = staged[768 + block * 8 : 768 + block * 8 + 8, :]
+        at = (63 - block) * 16
+        out_ref[at : at + 16, :] = south[block * 16 : block * 16 + 16, :]
 
 
 def grid_kernel(
     in_ref, choice_ref, weight_ref, synth_h, synth_l, anal_h, anal_l, twiddle_ref, out_ref,
     coeff, spread, fields, back
 ):
-    columns = in_ref[...].T[:160]
+    columns = jnp.concatenate(
+        [in_ref[pl.ds(0, SLOTS, stride=2), :].T, in_ref[pl.ds(1, SLOTS, stride=2), :].T[:32]], axis=0
+    )
     high, low = split(columns)
     picked = jnp.dot(
         jnp.concatenate([high, low], axis=0), choice_ref[...], preferred_element_type=F32
@@ -210,24 +209,21 @@
     high, low = split(back[...])
     across = (((1,), (1,)), ((), ()))
     choice = choice_ref[...]
-    out_ref[:, 0:160] = lax.dot_general(
+    message = lax.dot_general(
         choice, high, across, preferred_element_type=F32
     ) + lax.dot_general(choice, low, across, preferred_element_type=F32)
-    out_ref[:, 160:256] = jnp.zeros((SLOTS, 96), F32)
-
-
-def analysis_kernel(slot_ref, pairs_ref, in_ref, table_ref, out_ref, turned, staged):
-    staged[0:256, :] = in_ref[0:256, 0:128]
-    staged[256:512, :] = in_ref[0:256, 128:256]
+    out_ref[pl.ds(0, SLOTS, stride=2), :] = message[:, 0:128]
+    out_ref[pl.ds(1, SLOTS, stride=2), 0:32] = message[:, 128:160]
+
+
+def analysis_kernel(slot_ref, pairs_ref, in_ref, table_ref, out_ref, turned, south):
     for block in range(32):
-        at = (63 - block) * 8
-        staged[512 + block * 8 : 512 + block * 8 + 8, :] = in_ref[at : at + 8, 0:128]
-        staged[768 + block * 8 : 768 + block * 8 + 8, :] = in_ref[at : at + 8, 128:256]
+        at = (63 - block) * 16
+        south[block * 16 : block * 16 + 16, :] = in_ref[at : at + 16, :]
     lane = lax.broadcasted_iota(jnp.int32, (128, 128), 1)
     left = lane < 64
-    north_a, north_b, south_a, south_b = (
-        [staged[pl.ds(256 * q + f, 128, stride=2), :] for f in range(2)] for q in range(4)
-    )
+    north_a, north_b = ([in_ref[pl.ds(2 * f + c, 128, stride=4), :] for f in range(2)] for c in range(2))
+    south_a, south_b = ([south[pl.ds(2 * f + c, 128, stride=4), :] for f in range(2)] for c in range(2))
     for f in range(2):
         turned[pl.ds(3 * f, 128, stride=5), :] = jnp.where(
             left, north_a[f], pltpu.roll(south_a[f], 64, 1)
@@ -277,7 +273,7 @@
 
 
 def legendre_scratch():
-    return [pltpu.VMEM((HALF, 128), F32), pltpu.VMEM((1024, 128), F32)]
+    return [pltpu.VMEM((HALF, 128), F32), pltpu.VMEM((512, 128), F32)]
 
 
 def slot_choice(slot_pair):
@@ -311,7 +307,7 @@
     slot = (band * lons + lon).astype(jnp.int32).reshape(1)
     outgoing = pl.pallas_call(
         synthesis_kernel,
-        out_shape=jax.ShapeDtypeStruct((SLOTS, 256), F32),
+        out_shape=jax.ShapeDtypeStruct((2 * SLOTS, 128), F32),
         in_specs=[SMEM, SMEM, VMEM, VMEM],
         out_specs=VMEM,
         scratch_shapes=legendre_scratch(),
@@ -319,14 +315,14 @@
         name="legendre_synthesis",
     )(slot, slot_pair, spectral_in, leg_synthesis)
     arrived = lax.all_to_all(
-        outgoing.reshape(SLOTS, 1, 256), ("band", "lon"), split_axis=0, concat_axis=0, tiled=True
-    ).reshape(SLOTS, 256)
+        outgoing.reshape(SLOTS, 2, 128), ("band", "lon"), split_axis=0, concat_axis=0, tiled=True
+    ).reshape(2 * SLOTS, 128)
     choice = slot_choice(slot_pair)
     weights = advection_weights(departure_cells, departure_frac, band, lon, bands)
     (synth_h, synth_l), (anal_h, anal_l), twiddle = fine_tables()
     returning = pl.pallas_call(
         grid_kernel,
-        out_shape=jax.ShapeDtypeStruct((SLOTS, 256), F32),
+        out_shape=jax.ShapeDtypeStruct((2 * SLOTS, 128), F32),
         in_specs=[VMEM] * 8,
         out_specs=VMEM,
         scratch_shapes=[
@@ -339,8 +335,8 @@
         name="grid_step",
     )(arrived, choice, weights, synth_h, synth_l, anal_h, anal_l, twiddle)
     returned = lax.all_to_all(
-        returning.reshape(SLOTS, 1, 256), ("band", "lon"), split_axis=0, concat_axis=0, tiled=True
-    ).reshape(SLOTS, 256)
+        returning.reshape(SLOTS, 2, 128), ("band", "lon"), split_axis=0, concat_axis=0, tiled=True
+    ).reshape(2 * SLOTS, 128)
     return pl.pallas_call(
         analysis_kernel,
         out_shape=jax.ShapeDtypeStruct((1, 32, ROWS), F32),

time: 89.9 us -> 88.2 us (0.981)
  local copies, waits for them, and re-layouts: 10.2 us -> 7.42 us
  starting transfers between devices: 32.7 us -> 30.6 us
  waiting for transfers between devices: 38 us -> 40 us
  Pallas kernels: 7.72 us -> 9.04 us
    reshape x2 -> x0, local copies, waits for them, and re-layouts: 2.67 us -> none  [the longest x1 1.34 us: per_device(): returning.reshape(SLOTS, 1, 256)]
    all_to_all x2, starting transfers between devices: 32.7 us -> 30.6 us  [the longest x1 22.2 us: per_device(): lax.all_to_all(outgoing.reshape(SLOTS, 2, 128), ('band', 'lon'), split_ax...]
    all_to_all x2, waiting for transfers between devices: 38 us -> 40 us  [the longest x1 20.6 us: per_device(): lax.all_to_all(outgoing.reshape(SLOTS, 2, 128), ('band', 'lon'), split_ax...]
    pallas_call x2, Pallas kernels: 5.44 us -> 6.82 us  [the longest x1 4.54 us: per_device(): pl.pallas_call(grid_kernel, out_shape=jax.ShapeDtypeStruct((2 * SLOTS, 12...]
    unnamed x22 -> x20, local copies, waits for them, and re-layouts: 6.2 us -> 6.08 us
where the time goes in v2:
time: 88.2 us; the launch traced here: 87.9 us
  waiting for transfers between devices  40 us (45%)
  starting transfers between devices  30.6 us (35%)
  Pallas kernels  9.04 us (10%)
  local copies, waits for them, and re-layouts  7.42 us (8%)
    all_to_all x1, starting transfers between devices, per_device(): lax.all_to_all(outgoing.reshape(SLOTS, 2, 128), ('band', 'lon'), split_ax...  22.2 us
    all_to_all x1, waiting for transfers between devices, per_device(): lax.all_to_all(outgoing.reshape(SLOTS, 2, 128), ('band', 'lon'), split_ax...  20.6 us
    all_to_all x1, waiting for transfers between devices, per_device(): lax.all_to_all(returning.reshape(SLOTS, 2, 128), ('band', 'lon'), split_a...  19.4 us
    all_to_all x1, starting transfers between devices, per_device(): lax.all_to_all(returning.reshape(SLOTS, 2, 128), ('band', 'lon'), split_a...  8.45 us
    unnamed x20, local copies, waits for them, and re-layouts  6.08 us
    pallas_call x1, Pallas kernels, per_device(): pl.pallas_call(grid_kernel, out_shape=jax.ShapeDtypeStruct((2 * SLOTS, 12...  4.54 us
    pallas_call x1, Pallas kernels, per_device(): pl.pallas_call(synthesis_kernel, out_shape=jax.ShapeDtypeStruct((2 * SLOT...  2.28 us
    pallas_call x1, Pallas kernels, per_device(): pl.pallas_call(analysis_kernel, out_shape=jax.ShapeDtypeStruct((1, 32, RO...  2.22 us
  transfers between devices with their start and end apart: 2, of which 2 were waited for; matrix products, arithmetic and copies ran while one was open for 6% of the time, Pallas kernels for 0%

profile of v2, /device:TPU:1, one launch (start us, length us, event | category | flops | bytes accessed | tf_op | source)
XLA Modules:
  0.0 87.9 jit_solution(10897043659793098547)
XLA Ops:
  0.0 1.6 %copy.12.table_ref = f32[1,641,640]{2,1,0:T(8,128)S(1)} copy(f32[1,641,640]{2,0,1:T(1,128)} %param.12) | data formatting | bytes 3281920 | tf_op args[1]
  1.6 0.0 copy-start.8
  1.6 2.3 %legendre_synthesis.1 = f32[1024,128]{1,0:T(8,128)} custom-call(s32[1]{0:T(128)} %bitcast.slot_ref, s32[512]{0:T(512)S(1)} %copy-done.7, f32[1,32,641]{2,1,0:T(8,128)S(1)} %copy-done.5, f32[1,641,640]{2,1,0:T(8,128)S(1)} %copy.12.table_ref), custom_call_target="tpu_custom_call" | custom-call | tf_op jit(solution)/shard_map/legendre_synthesis/pallas_call | solution.py:308
  3.9 22.2 %all-to-all-start = ((f32[512,2,128]{2,1,0:T(2,128)}), f32[512,2,128]{2,1,0:T(2,128)S(1)}, u32[]{:S(2)}, u32[]{:S(2)}) async-start(f32[512,2,128]{2,1,0:T(2,128)} %bitcast.1), calls=%async_computation | async-start | bytes 1048576 | tf_op jit(solution)/shard_map/all_to_all | solution.py:317
  26.2 0.6 gather_fusion.1
  26.8 0.1 gather.15
  26.9 0.0 copy-start.1
  26.9 0.0 copy-start.2
  26.9 0.0 copy-start.3
  26.9 0.0 copy-start.6
  26.9 0.6 gather_fusion
  27.5 0.1 gather.13
  27.6 0.1 broadcast_select_fusion.1
  27.6 0.1 broadcast_subtract_fusion
  27.7 0.2 select_add_fusion
  28.0 0.2 compare_convert_fusion.choice_ref
  28.2 20.6 %all-to-all-done = f32[512,2,128]{2,1,0:T(2,128)S(1)} async-done(((f32[512,2,128]{2,1,0:T(2,128)}), f32[512,2,128]{2,1,0:T(2,128)S(1)}, u32[]{:S(2)}, u32[]{:S(2)}) %all-to-all-start) | async-done | bytes 524320 | tf_op jit(solution)/shard_map/all_to_all | solution.py:317
  48.8 0.0 copy-start.4
  48.9 1.0 %copy-done.4 = bf16[768,256]{1,0:T(8,128)(2,1)S(1)} copy-done((bf16[768,256]{1,0:T(8,128)(2,1)S(1)}, bf16[768,256]{1,0:T(8,128)(2,1)}, u32[]{:S(2)}) %copy-start.4) | copy-done | bytes 393240
  49.8 4.5 %grid_step.1 = f32[1024,128]{1,0:T(8,128)} custom-call(f32[1024,128]{1,0:T(8,128)S(1)} %bitcast.8, bf16[512,1024]{1,0:T(8,128)(2,1)S(1)} %compare_convert_fusion.choice_ref, f32[5,8,5,384]{3,2,1,0:T(8,128)S(1)} %pad.4.weight_ref, bf16[256,768]{1,0:T(8,128)(2,1)S(1)} %copy-done.1, bf16[256,768]{1,0:T(8,128)(2,1)S(1)} %copy-done.2, ...), custom_call_target="tpu_custom_call" | custom-call | tf_op jit(solution)/shard_map/grid_step/pallas_call | solution.py:323
  54.4 8.4 %all-to-all-start.1 = ((f32[512,2,128]{2,1,0:T(2,128)}), f32[512,2,128]{2,1,0:T(2,128)S(1)}, u32[]{:S(2)}, u32[]{:S(2)}) async-start(f32[512,2,128]{2,1,0:T(2,128)} %bitcast.4), calls=%async_computation.1 | async-start | bytes 1048576 | tf_op jit(solution)/shard_map/all_to_all | solution.py:337
  62.8 3.5 %copy.13.table_ref = f32[1,640,641]{2,1,0:T(8,128)S(1)} copy(f32[1,640,641]{1,0,2:T(1,128)} %param.13) | data formatting | bytes 3281920 | tf_op args[2]
  66.3 19.4 %all-to-all-done.1 = f32[512,2,128]{2,1,0:T(2,128)S(1)} async-done(((f32[512,2,128]{2,1,0:T(2,128)}), f32[512,2,128]{2,1,0:T(2,128)S(1)}, u32[]{:S(2)}, u32[]{:S(2)}) %all-to-all-start.1) | async-done | bytes 524320 | tf_op jit(solution)/shard_map/all_to_all | solution.py:337
  85.7 2.2 %legendre_analysis.1 = f32[1,32,641]{2,1,0:T(8,128)} custom-call(s32[1]{0:T(128)} %bitcast.slot_ref, s32[512]{0:T(512)S(1)} %copy-done.7, f32[1024,128]{1,0:T(8,128)S(1)} %bitcast.7, f32[1,640,641]{2,1,0:T(8,128)S(1)} %copy.13.table_ref), custom_call_target="tpu_custom_call" | custom-call | tf_op jit(solution)/shard_map/legendre_analysis/pallas_call | solution.py:340
  (17 shorter events, 0.1 us)
Async XLA Ops:
  0.0 26.2 %copy-start = (f32[20,2560]{1,0:T(8,128)S(1)}, f32[20,2560]{1,0:T(8,128)}, u32[]{:S(2)}) copy-start(f32[20,2560]{1,0:T(8,128)} %param.16) | copy-start | bytes 614404
  0.0 1.6 %copy-start.7 = (s32[512]{0:T(512)S(1)}, s32[512]{0:T(512)}, u32[]{:S(2)}) copy-start(s32[512]{0:T(512)} %pairs_ref.3) | copy-start | bytes 6148
  0.0 1.6 %copy-start.5 = (f32[1,32,641]{2,1,0:T(8,128)S(1)}, f32[1,32,641]{2,1,0:T(8,128)}, u32[]{:S(2)}) copy-start(f32[1,32,641]{2,1,0:T(8,128)} %spec_ref.1) | copy-start | bytes 246148
  1.6 25.2 %copy-start.8 = (s32[20,2560]{1,0:T(8,128)S(1)}, s32[20,2560]{1,0:T(8,128)}, u32[]{:S(2)}) copy-start(s32[20,2560]{1,0:T(8,128)} %param.15) | copy-start | bytes 614404
  3.9 44.9 %all-to-all-start = ((f32[512,2,128]{2,1,0:T(2,128)}), f32[512,2,128]{2,1,0:T(2,128)S(1)}, u32[]{:S(2)}, u32[]{:S(2)}) async-start(f32[512,2,128]{2,1,0:T(2,128)} %bitcast.1), calls=%async_computation | async-start | bytes 1048576 | tf_op jit(solution)/shard_map/all_to_all | solution.py:317
  26.9 22.0 %copy-start.1 = (bf16[256,768]{1,0:T(8,128)(2,1)S(1)}, bf16[256,768]{1,0:T(8,128)(2,1)}, u32[]{:S(2)}) copy-start(bf16[256,768]{1,0:T(8,128)(2,1)} %constant.132.clone.synth_h) | copy-start | bytes 1179652
  26.9 21.9 %copy-start.2 = (bf16[256,768]{1,0:T(8,128)(2,1)S(1)}, bf16[256,768]{1,0:T(8,128)(2,1)}, u32[]{:S(2)}) copy-start(bf16[256,768]{1,0:T(8,128)(2,1)} %constant.133.clone.synth_l) | copy-start | bytes 1179652
  26.9 21.9 %copy-start.3 = (bf16[768,256]{1,0:T(8,128)(2,1)S(1)}, bf16[768,256]{1,0:T(8,128)(2,1)}, u32[]{:S(2)}) copy-start(bf16[768,256]{1,0:T(8,128)(2,1)} %constant.134.clone.anal_h) | copy-start | bytes 1179652
  26.9 21.9 %copy-start.6 = (f32[16,384]{1,0:T(8,128)S(1)}, f32[16,384]{1,0:T(8,128)}, u32[]{:S(2)}) copy-start(f32[16,384]{1,0:T(8,128)} %constant.136.clone.twiddle_ref) | copy-start | bytes 73732
  48.8 1.0 %copy-start.4 = (bf16[768,256]{1,0:T(8,128)(2,1)S(1)}, bf16[768,256]{1,0:T(8,128)(2,1)}, u32[]{:S(2)}) copy-start(bf16[768,256]{1,0:T(8,128)(2,1)} %constant.135.clone.anal_l) | copy-start | bytes 1179652
  54.4 31.3 %all-to-all-start.1 = ((f32[512,2,128]{2,1,0:T(2,128)}), f32[512,2,128]{2,1,0:T(2,128)S(1)}, u32[]{:S(2)}, u32[]{:S(2)}) async-start(f32[512,2,128]{2,1,0:T(2,128)} %bitcast.4), calls=%async_computation.1 | async-start | bytes 1048576 | tf_op jit(solution)/shard_map/all_to_all | solution.py:337

commit v3 on v2

v3 whole, which is shorter than its diff:
```python
import math

import jax
import jax.numpy as jnp
import ml_dtypes
import numpy as np
from jax import lax
from jax.experimental import pallas as pl
from jax.experimental.pallas import tpu as pltpu
from jax.sharding import PartitionSpec as P

WAVES = 640
PAIRS = 320
ROWS = 641
HALF = 640
NLON = 2560
SLOTS = 512
RADIX = 10
FINE = 64
SEG = 256
HALF_ROWS = 5
REACH = 4
BF = jnp.bfloat16
F32 = jnp.float32


def halves(table):
    high = table.astype(np.float32).astype(ml_dtypes.bfloat16)
    low = (table - high.astype(np.float64)).astype(np.float32).astype(ml_dtypes.bfloat16)
    return high, low


def fine_tables():
    place = np.arange(SEG)
    phase = 2 * math.pi * ((np.arange(FINE)[:, None] * place[None, :]) % SEG) / SEG
    cos, sin = np.cos(phase), np.sin(phase)
    synth = np.block([[2 * cos, 2 * sin], [-2 * sin, 2 * cos]])
    high, low = halves(synth)
    anal_high, anal_low = halves(synth.T / (2 * NLON))
    turn = 2 * math.pi * ((np.arange(RADIX)[:, None] * place[None, :]) % NLON) / NLON
    twiddle = np.concatenate([np.cos(turn), np.sin(turn)], axis=0).astype(np.float32)
    return (
        np.concatenate([high, high, low], axis=0),
        np.concatenate([anal_high, anal_low], axis=1),
        twiddle,
    )


def split(value):
    high = value.astype(BF)
    return high, (value - high.astype(F32)).astype(BF)


def dot3(left, right_high, right_low):
    high, low = split(left)
    rows = left.shape[0]
    both = jnp.dot(
        jnp.concatenate([high, low], axis=0), right_high, preferred_element_type=F32
    )
    return both[:rows] + both[rows:] + jnp.dot(high, right_low, preferred_element_type=F32)


def wave_rows(pair):
    row = lax.broadcasted_iota(jnp.int32, (1, ROWS), 1)
    cut = WAVES - pair
    upper = row < cut
    odd = jnp.where(upper, row, row - cut) & 1
    return upper, odd


def own_pair(pairs_ref):
    slot = lax.axis_index("band") * lax.axis_size("lon") + lax.axis_index("lon")
    shape = pairs_ref.shape
    index = lax.broadcasted_iota(jnp.int32, shape, 0) * shape[1] + lax.broadcasted_iota(
        jnp.int32, shape, 1
    )
    mine = jnp.where(index == slot, pairs_ref[...], 0)
    return jnp.sum(jnp.sum(mine, axis=1, keepdims=True), axis=0, keepdims=True)


def synthesis_kernel(pairs_ref, spec_ref, table_ref, out_ref, turned, south):
    pair = own_pair(pairs_ref)
    upper, odd = wave_rows(pair)
    live = pair < PAIRS
    groups = []
    for parity in range(2):
        for half in range(2):
            for wave in range(2):
                mask = jnp.logical_and(upper if wave == 0 else jnp.logical_not(upper), odd == parity)
                mask = jnp.logical_and(mask, live)
                for part in range(2):
                    first = part * 16 + half * 8
                    groups.append(jnp.where(mask, spec_ref[0, first : first + 8, :], 0.0))
    table_high, table_low = split(table_ref[0])
    product = dot3(jnp.concatenate(groups, axis=0), table_high, table_low)
    even, odd_sum = product[:64], product[64:]
    turned[...] = jnp.concatenate([even + odd_sum, even - odd_sum], axis=0).T
    lane = lax.broadcasted_iota(jnp.int32, (128, 128), 1)
    left = lane < 64
    pick = [turned[pl.ds(u, 128, stride=5), :] for u in range(5)]
    rolled = [pltpu.roll(q, 64, 1) for q in pick]
    out_ref[pl.ds(0, 128, stride=4), :] = jnp.where(left, pick[0], rolled[1])
    out_ref[pl.ds(1, 128, stride=4), :] = pick[2]
    out_ref[pl.ds(2, 128, stride=4), :] = jnp.where(left, pick[3], rolled[4])
    out_ref[pl.ds(3, 128, stride=4), :] = pltpu.roll(pick[2], 96, 1)
    south[pl.ds(0, 128, stride=4), :] = jnp.where(left, rolled[0], pick[1])
    south[pl.ds(1, 128, stride=4), :] = rolled[2]
    south[pl.ds(2, 128, stride=4), :] = jnp.where(left, rolled[3], pick[4])
    south[pl.ds(3, 128, stride=4), :] = pltpu.roll(pick[2], 32, 1)
    for block in range(32):
        at = (63 - block) * 16
        out_ref[at : at + 16, :] = south[block * 16 : block * 16 + 16, :]


def circle(degrees):
    return math.cos(math.radians(degrees)), math.sin(math.radians(degrees))


COS36, SIN36 = circle(36)
COS72, SIN72 = circle(72)


def to_segments(real, imag):
    p1, p2 = real[2] + real[8], real[4] + real[6]
    n1, n2 = imag[2] - imag[8], imag[4] - imag[6]
    a1, b1 = real[0] + COS72 * p1 - COS36 * p2, SIN72 * n1 + SIN36 * n2
    a2, b2 = real[0] - COS36 * p1 + COS72 * p2, SIN36 * n1 - SIN72 * n2
    evens = [real[0] + p1 + p2, a1 - b1, a2 - b2, a2 + b2, a1 + b1]
    q1, q3 = real[1] + real[9], real[3] + real[7]
    h1, h3 = imag[1] - imag[9], imag[3] - imag[7]
    a1, b1 = COS36 * q1 - COS72 * q3 - real[5], SIN36 * h1 + SIN72 * h3
    a2, b2 = real[5] + COS72 * q1 - COS36 * q3, SIN72 * h1 - SIN36 * h3
    odds = [real[5] + q1 + q3, a1 - b1, a2 - b2, -a2 - b2, -a1 - b1]
    return [e + o for e, o in zip(evens, odds)] + [e - o for e, o in zip(evens, odds)]


def from_segments(parts):
    s = [parts[k] + parts[k + 5] for k in range(5)]
    d = [parts[k] - parts[k + 5] for k in range(5)]
    p1, p2, n1, n2 = s[1] + s[4], s[2] + s[3], s[1] - s[4], s[2] - s[3]
    q1, q2, h1, h2 = d[1] - d[4], d[2] - d[3], d[1] + d[4], d[2] + d[3]
    return [
        (s[0] + p1 + p2, None),
        (d[0] + COS36 * q1 + COS72 * q2, -SIN36 * h1 - SIN72 * h2),
        (s[0] + COS72 * p1 - COS36 * p2, -SIN72 * n1 - SIN36 * n2),
        (d[0] - COS72 * q1 - COS36 * q2, SIN36 * h2 - SIN72 * h1),
        (s[0] - COS36 * p1 + COS72 * p2, SIN72 * n2 - SIN36 * n1),
        (d[0] - q1 + q2, None),
    ]


def grid_kernel(
    in_ref, choice_ref, weight_ref, synth_ref, anal_ref, twiddle_ref, out_ref,
    coeff, spread, fields, back
):
    columns = jnp.concatenate(
        [in_ref[pl.ds(0, SLOTS, stride=2), :].T, in_ref[pl.ds(1, SLOTS, stride=2), :].T[:32]], axis=0
    )
    choice = choice_ref[...]
    picked = jnp.dot(
        jnp.concatenate(split(columns), axis=0), choice, preferred_element_type=F32
    )
    lane = lax.broadcasted_iota(jnp.int32, (8, 128), 1)
    left = lane < FINE
    first_wave = (lane & (FINE - 1)) < FINE // 2
    mean_scale = jnp.where((lane & (FINE - 1)) == 0, 0.5, 1.0)
    for level in range(2):
        for i in range(HALF_ROWS):
            for q in range(RADIX // 2):
                base, cols = level * 160 + i * 32, slice(q * 128, q * 128 + 128)
                real = jnp.where(
                    first_wave, picked[base : base + 8, cols], picked[base + 16 : base + 24, cols]
                )
                imag = jnp.where(
                    first_wave, picked[base + 8 : base + 16, cols], picked[base + 24 : base + 32, cols]
                )
                even = jnp.where(left, real, pltpu.roll(imag, 64, 1))
                odd = jnp.where(left, pltpu.roll(real, 64, 1), imag)
                if q == 0:
                    even = even * mean_scale
                at = i * 80 + q * 16
                coeff[at : at + 8, level * 128 : level * 128 + 128] = even
                coeff[at + 8 : at + 16, level * 128 : level * 128 + 128] = odd
    both = coeff[...].astype(BF)
    spread[...] = jnp.dot(
        jnp.concatenate([both, both[:, :128]], axis=1), synth_ref[...], preferred_element_type=F32
    )
    for i in range(HALF_ROWS):
        real, imag = [], []
        for r in range(RADIX):
            at = i * 80 + r * 8
            zr, zi = spread[at : at + 8, :SEG], spread[at : at + 8, SEG:]
            if r == 0:
                real.append(zr)
                imag.append(None)
                continue
            tr, ti = twiddle_ref[r : r + 1, :], twiddle_ref[RADIX + r : RADIX + r + 1, :]
            real.append(tr * zr - ti * zi)
            imag.append(None if r == 5 else tr * zi + ti * zr)
        value = jnp.concatenate(to_segments(real, imag), axis=1)
        moved = weight_ref[i, 0:1, :] * value
        for offset in range(1, REACH + 1):
            moved = moved + weight_ref[i, offset : offset + 1, :] * pltpu.roll(value, offset, 1)
        waves = from_segments([moved[:, k * SEG : k * SEG + SEG] for k in range(RADIX)])
        for r in range(RADIX):
            vr, vi = waves[r] if r < 6 else waves[RADIX - r]
            if r > 5:
                vi = -vi
            at = i * 80 + r * 8
            if r == 0:
                fields[at : at + 8, :SEG] = vr
                fields[at : at + 8, SEG:] = jnp.zeros_like(vr)
                continue
            tr, ti = twiddle_ref[r : r + 1, :], twiddle_ref[RADIX + r : RADIX + r + 1, :]
            if vi is None:
                fields[at : at + 8, :SEG] = tr * vr
                fields[at : at + 8, SEG:] = -ti * vr
            else:
                fields[at : at + 8, :SEG] = tr * vr + ti * vi
                fields[at : at + 8, SEG:] = tr * vi - ti * vr
    wide = jnp.dot(
        jnp.concatenate(split(fields[...]), axis=0), anal_ref[...], preferred_element_type=F32
    )
    result = wide[:400, :128] + wide[:400, 128:] + wide[400:, :128]
    for i in range(HALF_ROWS):
        for q in range(RADIX // 2):
            at, cols = i * 80 + q * 16, slice(q * 128, q * 128 + 128)
            even, odd = result[at : at + 8], result[at + 8 : at + 16]
            real = jnp.where(left, even, pltpu.roll(odd, 64, 1))
            imag = jnp.where(left, pltpu.roll(even, 64, 1), odd)
            base = i * 32
            back[base : base + 8, cols] = jnp.where(first_wave, real, 0.0)
            back[base + 8 : base + 16, cols] = jnp.where(first_wave, imag, 0.0)
            back[base + 16 : base + 24, cols] = jnp.where(first_wave, 0.0, real)
            back[base + 24 : base + 32, cols] = jnp.where(first_wave, 0.0, imag)
    sent = lax.dot_general(
        jnp.concatenate(split(back[...]), axis=0), choice, (((1,), (1,)), ((), ())),
        preferred_element_type=F32,
    )
    sent = sent[:160] + sent[160:]
    out_ref[pl.ds(0, SLOTS, stride=2), :] = sent[:128].T
    out_ref[pl.ds(1, SLOTS, stride=2), 0:32] = sent[128:].T


def analysis_kernel(pairs_ref, in_ref, table_ref, out_ref, turned, south):
    for block in range(32):
        at = (63 - block) * 16
        south[block * 16 : block * 16 + 16, :] = in_ref[at : at + 16, :]
    lane = lax.broadcasted_iota(jnp.int32, (128, 128), 1)
    left = lane < 64
    north_a, north_b = ([in_ref[pl.ds(2 * f + c, 128, stride=4), :] for f in range(2)] for c in range(2))
    south_a, south_b = ([south[pl.ds(2 * f + c, 128, stride=4), :] for f in range(2)] for c in range(2))
    for f in range(2):
        turned[pl.ds(3 * f, 128, stride=5), :] = jnp.where(
            left, north_a[f], pltpu.roll(south_a[f], 64, 1)
        )
        turned[pl.ds(3 * f + 1, 128, stride=5), :] = jnp.where(
            left, pltpu.roll(north_a[f], 64, 1), south_a[f]
        )
    turned[pl.ds(2, 128, stride=5), :] = jnp.where(
        left,
        jnp.where(lane < 32, north_b[0], pltpu.roll(north_b[1], 32, 1)),
        jnp.where(lane < 96, pltpu.roll(south_b[0], 64, 1), pltpu.roll(south_b[1], 96, 1)),
    )
    straight = turned[...].T
    north, south_rows = straight[:64], straight[64:]
    table_high, table_low = split(table_ref[0])
    product = dot3(
        jnp.concatenate([north + south_rows, north - south_rows], axis=0), table_high, table_low
    )
    pair = own_pair(pairs_ref)
    upper, odd = wave_rows(pair)
    live = pair < PAIRS
    even = odd == 0
    for half in range(2):
        for part in range(2):
            rows = [
                [
                    product[
                        parity * 64 + half * 32 + wave * 16 + part * 8 :
                        parity * 64 + half * 32 + wave * 16 + part * 8 + 8
                    ]
                    for parity in range(2)
                ]
                for wave in range(2)
            ]
            value = jnp.where(
                upper,
                jnp.where(even, rows[0][0], rows[0][1]),
                jnp.where(even, rows[1][0], rows[1][1]),
            )
            first = part * 16 + half * 8
            out_ref[0, first : first + 8, :] = jnp.where(live, value, 0.0)


VMEM = pl.BlockSpec(memory_space=pltpu.VMEM)
PARAMS = pltpu.CompilerParams(vmem_limit_bytes=40 * 1024 * 1024)


def slot_choice(slot_pair):
    column = jnp.arange(RADIX * FINE, dtype=jnp.int32)
    wave = (column % FINE) * RADIX + column // FINE
    pair = jnp.where(wave < PAIRS, wave, WAVES - 1 - wave)
    return (slot_pair[:, None] == pair[None, :]).astype(BF)


def advection_weights(cells, fraction, band, lon, bands):
    position = jnp.arange(HALF_ROWS, dtype=jnp.int32)
    position = jnp.where(lon % 2 == 0, position, (position + 1) % HALF_ROWS)
    row = (HALF_ROWS * lon + position) // 2
    row = jnp.where(band < bands // 2, row, cells.shape[0] - 1 - row)
    cells = jnp.take(cells, row, axis=0)[:, None, :]
    fraction = jnp.take(fraction, row, axis=0)[:, None, :]
    offset = jnp.arange(REACH + 1, dtype=jnp.int32)[None, :, None]
    return jnp.where(cells == offset, 1.0 - fraction, 0.0) + jnp.where(
        cells == offset - 1, fraction, 0.0
    )


def legendre_synthesis(slot_pair, spectral_in, leg_synthesis):
    return pl.pallas_call(
        synthesis_kernel,
        out_shape=jax.ShapeDtypeStruct((2 * SLOTS, 128), F32),
        in_specs=[VMEM] * 3,
        out_specs=VMEM,
        scratch_shapes=[
            pltpu.VMEM((HALF, 128), F32),
            pltpu.VMEM((SLOTS, 128), F32),
        ],
        compiler_params=PARAMS,
        name="legendre_synthesis",
    )(slot_pair.reshape(-1, 128), spectral_in, leg_synthesis)


def grid_step(arrived, choice, weights):
    return pl.pallas_call(
        grid_kernel,
        out_shape=jax.ShapeDtypeStruct((2 * SLOTS, 128), F32),
        in_specs=[VMEM] * 6,
        out_specs=VMEM,
        scratch_shapes=[
            pltpu.VMEM((400, 256), F32),
            pltpu.VMEM((400, 2 * SEG), F32),
            pltpu.VMEM((400, 2 * SEG), F32),
            pltpu.VMEM((160, WAVES), F32),
        ],
        compiler_params=PARAMS,
        name="grid_step",
    )(arrived, choice, weights, *fine_tables())


def legendre_analysis(slot_pair, returned, leg_analysis):
    return pl.pallas_call(
        analysis_kernel,
        out_shape=jax.ShapeDtypeStruct((1, 32, ROWS), F32),
        in_specs=[VMEM] * 3,
        out_specs=VMEM,
        scratch_shapes=[pltpu.VMEM((HALF, 128), F32), pltpu.VMEM((SLOTS, 128), F32)],
        compiler_params=PARAMS,
        name="legendre_analysis",
    )(slot_pair.reshape(-1, 128), returned, leg_analysis)


def exchange(messages):
    return lax.all_to_all(
        messages.reshape(SLOTS, 2, 128), ("band", "lon"), split_axis=0, concat_axis=0, tiled=True
    ).reshape(2 * SLOTS, 128)


def per_device(
    spectral_in, leg_synthesis, leg_analysis, slot_pair, departure_cells, departure_frac
):
    arrived = exchange(legendre_synthesis(slot_pair, spectral_in, leg_synthesis))
    choice = slot_choice(slot_pair)
    weights = advection_weights(
        departure_cells, departure_frac, lax.axis_index("band"), lax.axis_index("lon"),
        lax.axis_size("band"),
    )
    returned = exchange(grid_step(arrived, choice, weights))
    return legendre_analysis(slot_pair, returned, leg_analysis)


def solution(mesh):
    return jax.shard_map(
        per_device,
        mesh=mesh,
        in_specs=(
            P(("band", "lon"), None, None),
            P(("band", "lon"), None, None),
            P(("band", "lon"), None, None),
            P(),
            P("band", None),
            P("band", None),
        ),
        out_specs=P(("band", "lon"), None, None),
        check_vma=False,
    )
```

time: 88.2 us -> 85.2 us (0.966)
  Pallas kernels: 9.04 us -> 7.11 us
  local copies, waits for them, and re-layouts: 7.42 us -> 6.22 us
    pallas_call x3, Pallas kernels: 9.04 us -> 7.11 us  [the longest x1 3.55 us: grid_step(): pl.pallas_call(grid_kernel, out_shape=jax.ShapeDtypeStruct((2 * SLOTS, 12...]
    unnamed x20 -> x16, local copies, waits for them, and re-layouts: 6.08 us -> 5.08 us
where the time goes in v3:
time: 85.2 us; the launch traced here: 84.9 us
  waiting for transfers between devices  40.1 us (47%)
  starting transfers between devices  30.7 us (36%)
  Pallas kernels  7.11 us (8%)
  local copies, waits for them, and re-layouts  6.22 us (7%)
    all_to_all x2, waiting for transfers between devices, exchange(): lax.all_to_all(messages.reshape(SLOTS, 2, 128), ('band', 'lon'), split_ax...  40.1 us
    all_to_all x2, starting transfers between devices, exchange(): lax.all_to_all(messages.reshape(SLOTS, 2, 128), ('band', 'lon'), split_ax...  30.7 us
    unnamed x16, local copies, waits for them, and re-layouts  5.08 us
    pallas_call x1, Pallas kernels, grid_step(): pl.pallas_call(grid_kernel, out_shape=jax.ShapeDtypeStruct((2 * SLOTS, 12...  3.55 us
    pallas_call x1, Pallas kernels, legendre_synthesis(): pl.pallas_call(synthesis_kernel, out_shape=jax.ShapeDtypeStruct((2 * SLOT...  1.84 us
    pallas_call x1, Pallas kernels, legendre_analysis(): pl.pallas_call(analysis_kernel, out_shape=jax.ShapeDtypeStruct((1, 32, RO...  1.72 us
  transfers between devices with their start and end apart: 2, of which 2 were waited for; matrix products, arithmetic and copies ran while one was open for 6% of the time, Pallas kernels for 0%

profile of v3, /device:TPU:1, one launch (start us, length us, event | category | flops | bytes accessed | tf_op | source)
XLA Modules:
  0.0 84.9 jit_solution(2180216289533939028)
XLA Ops:
  0.0 0.0 copy-start
  0.0 1.6 %copy.10.table_ref = f32[1,641,640]{2,1,0:T(8,128)S(1)} copy(f32[1,641,640]{2,0,1:T(1,128)} %param.10) | data formatting | bytes 3281920 | tf_op args[1]
  1.6 0.0 copy-done.5
  1.6 0.0 copy-done.3
  1.6 0.0 copy-start.6
  1.6 1.8 %legendre_synthesis.1 = f32[1024,128]{1,0:T(8,128)} custom-call(s32[4,128]{1,0:T(4,128)S(1)} %bitcast.9, f32[1,32,641]{2,1,0:T(8,128)S(1)} %copy-done.3, f32[1,641,640]{2,1,0:T(8,128)S(1)} %copy.10.table_ref), custom_call_target="tpu_custom_call" | custom-call | tf_op jit(solution)/shard_map/legendre_synthesis/pallas_call | solution.py:321
  3.5 22.2 %all-to-all-start = ((f32[512,2,128]{2,1,0:T(2,128)}), f32[512,2,128]{2,1,0:T(2,128)S(1)}, u32[]{:S(2)}, u32[]{:S(2)}) async-start(f32[512,2,128]{2,1,0:T(2,128)} %bitcast.1), calls=%async_computation | async-start | bytes 1048576 | tf_op jit(solution)/shard_map/all_to_all | solution.py:365
  25.6 0.0 copy-start.1
  25.7 0.0 copy-start.2
  25.7 0.0 copy-start.4
  25.8 0.0 copy-done
  25.8 0.6 gather_fusion.1
  26.4 0.6 gather_fusion
  26.9 0.1 broadcast_subtract_fusion
  27.0 0.1 broadcast_select_fusion.1
  27.1 0.2 compare_convert_fusion.choice_ref
  27.3 0.1 select_add_fusion.weight_ref
  27.5 20.8 %all-to-all-done = f32[512,2,128]{2,1,0:T(2,128)S(1)} async-done(((f32[512,2,128]{2,1,0:T(2,128)}), f32[512,2,128]{2,1,0:T(2,128)S(1)}, u32[]{:S(2)}, u32[]{:S(2)}) %all-to-all-start) | async-done | bytes 524320 | tf_op jit(solution)/shard_map/all_to_all | solution.py:365
  48.3 0.0 copy-done.2
  48.3 3.5 %grid_step.1 = f32[1024,128]{1,0:T(8,128)} custom-call(f32[1024,128]{1,0:T(8,128)S(1)} %bitcast.7, bf16[512,640]{1,0:T(8,128)(2,1)S(1)} %compare_convert_fusion.choice_ref, f32[5,5,2560]{2,1,0:T(8,128)S(1)} %select_add_fusion.weight_ref, bf16[384,512]{1,0:T(8,128)(2,1)S(1)} %copy-done.1, bf16[512,256]{1,0:T(8,128)(2,1)S(1)} %copy-done.2, f32[20,256]{1,0:T(8,128)S(1)} %copy-done.4), custom_call_target="tpu_custom_call" | custom-call | tf_op jit(solution)/shard_map/grid_step/pallas_call | solution.py:336
  51.8 8.6 %all-to-all-start.1 = ((f32[512,2,128]{2,1,0:T(2,128)}), f32[512,2,128]{2,1,0:T(2,128)S(1)}, u32[]{:S(2)}, u32[]{:S(2)}) async-start(f32[512,2,128]{2,1,0:T(2,128)} %bitcast.4), calls=%async_computation.1 | async-start | bytes 1048576 | tf_op jit(solution)/shard_map/all_to_all | solution.py:365
  60.4 3.5 %copy.11.table_ref = f32[1,640,641]{2,1,0:T(8,128)S(1)} copy(f32[1,640,641]{1,0,2:T(1,128)} %param.11) | data formatting | bytes 3281920 | tf_op args[2]
  63.9 19.3 %all-to-all-done.1 = f32[512,2,128]{2,1,0:T(2,128)S(1)} async-done(((f32[512,2,128]{2,1,0:T(2,128)}), f32[512,2,128]{2,1,0:T(2,128)S(1)}, u32[]{:S(2)}, u32[]{:S(2)}) %all-to-all-start.1) | async-done | bytes 524320 | tf_op jit(solution)/shard_map/all_to_all | solution.py:365
  83.2 1.7 %legendre_analysis.1 = f32[1,32,641]{2,1,0:T(8,128)} custom-call(s32[4,128]{1,0:T(4,128)S(1)} %bitcast.10, f32[1024,128]{1,0:T(8,128)S(1)} %bitcast.8, f32[1,640,641]{2,1,0:T(8,128)S(1)} %copy.11.table_ref), custom_call_target="tpu_custom_call" | custom-call | tf_op jit(solution)/shard_map/legendre_analysis/pallas_call | solution.py:353
  (10 shorter events, 0.1 us)
Async XLA Ops:
  0.0 25.8 %copy-start = (f32[20,2560]{1,0:T(8,128)S(1)}, f32[20,2560]{1,0:T(8,128)}, u32[]{:S(2)}) copy-start(f32[20,2560]{1,0:T(8,128)} %param.14) | copy-start | bytes 614404
  0.0 1.6 %copy-start.5 = (s32[512]{0:T(512)S(1)}, s32[512]{0:T(512)}, u32[]{:S(2)}) copy-start(s32[512]{0:T(512)} %param.12) | copy-start | bytes 6148
  0.0 1.6 %copy-start.3 = (f32[1,32,641]{2,1,0:T(8,128)S(1)}, f32[1,32,641]{2,1,0:T(8,128)}, u32[]{:S(2)}) copy-start(f32[1,32,641]{2,1,0:T(8,128)} %spec_ref.1) | copy-start | bytes 246148
  1.6 24.7 %copy-start.6 = (s32[20,2560]{1,0:T(8,128)S(1)}, s32[20,2560]{1,0:T(8,128)}, u32[]{:S(2)}) copy-start(s32[20,2560]{1,0:T(8,128)} %param.13) | copy-start | bytes 614404
  3.5 44.8 %all-to-all-start = ((f32[512,2,128]{2,1,0:T(2,128)}), f32[512,2,128]{2,1,0:T(2,128)S(1)}, u32[]{:S(2)}, u32[]{:S(2)}) async-start(f32[512,2,128]{2,1,0:T(2,128)} %bitcast.1), calls=%async_computation | async-start | bytes 1048576 | tf_op jit(solution)/shard_map/all_to_all | solution.py:365
  25.6 22.6 %copy-start.1 = (bf16[384,512]{1,0:T(8,128)(2,1)S(1)}, bf16[384,512]{1,0:T(8,128)(2,1)}, u32[]{:S(2)}) copy-start(bf16[384,512]{1,0:T(8,128)(2,1)} %constant.123.clone.synth_ref) | copy-start | bytes 1179652
  25.7 22.6 %copy-start.2 = (bf16[512,256]{1,0:T(8,128)(2,1)S(1)}, bf16[512,256]{1,0:T(8,128)(2,1)}, u32[]{:S(2)}) copy-start(bf16[512,256]{1,0:T(8,128)(2,1)} %constant.124.clone.anal_ref) | copy-start | bytes 786436
  25.7 22.6 %copy-start.4 = (f32[20,256]{1,0:T(8,128)S(1)}, f32[20,256]{1,0:T(8,128)}, u32[]{:S(2)}) copy-start(f32[20,256]{1,0:T(8,128)} %constant.125.clone.twiddle_ref) | copy-start | bytes 61444
  51.8 31.3 %all-to-all-start.1 = ((f32[512,2,128]{2,1,0:T(2,128)}), f32[512,2,128]{2,1,0:T(2,128)S(1)}, u32[]{:S(2)}, u32[]{:S(2)}) async-start(f32[512,2,128]{2,1,0:T(2,128)} %bitcast.4), calls=%async_computation.1 | async-start | bytes 1048576 | tf_op jit(solution)/shard_map/all_to_all | solution.py:365

commit v4 on v3

--- a/solution.py
+++ b/solution.py
@@ -78,7 +78,16 @@
     return jnp.sum(jnp.sum(mine, axis=1, keepdims=True), axis=0, keepdims=True)
 
 
-def synthesis_kernel(pairs_ref, spec_ref, table_ref, out_ref, turned, south):
+def backwards(value):
+    row = lax.broadcasted_iota(jnp.int32, (8, 128), 0)
+    parts = [
+        jnp.take_along_axis(value[at : at + 8], 7 - row, axis=0, mode="promise_in_bounds")
+        for at in range(value.shape[0] - 8, -1, -8)
+    ]
+    return jnp.concatenate(parts, axis=0)
+
+
+def synthesis_kernel(pairs_ref, spec_ref, table_ref, out_ref, turned):
     pair = own_pair(pairs_ref)
     upper, odd = wave_rows(pair)
     live = pair < PAIRS
@@ -95,21 +104,21 @@
     product = dot3(jnp.concatenate(groups, axis=0), table_high, table_low)
     even, odd_sum = product[:64], product[64:]
     turned[...] = jnp.concatenate([even + odd_sum, even - odd_sum], axis=0).T
-    lane = lax.broadcasted_iota(jnp.int32, (128, 128), 1)
+    lane = lax.broadcasted_iota(jnp.int32, (32, 128), 1)
     left = lane < 64
-    pick = [turned[pl.ds(u, 128, stride=5), :] for u in range(5)]
-    rolled = [pltpu.roll(q, 64, 1) for q in pick]
-    out_ref[pl.ds(0, 128, stride=4), :] = jnp.where(left, pick[0], rolled[1])
-    out_ref[pl.ds(1, 128, stride=4), :] = pick[2]
-    out_ref[pl.ds(2, 128, stride=4), :] = jnp.where(left, pick[3], rolled[4])
-    out_ref[pl.ds(3, 128, stride=4), :] = pltpu.roll(pick[2], 96, 1)
-    south[pl.ds(0, 128, stride=4), :] = jnp.where(left, rolled[0], pick[1])
-    south[pl.ds(1, 128, stride=4), :] = rolled[2]
-    south[pl.ds(2, 128, stride=4), :] = jnp.where(left, rolled[3], pick[4])
-    south[pl.ds(3, 128, stride=4), :] = pltpu.roll(pick[2], 32, 1)
-    for block in range(32):
-        at = (63 - block) * 16
-        out_ref[at : at + 16, :] = south[block * 16 : block * 16 + 16, :]
+    for g in range(4):
+        pick = [turned[pl.ds(5 * g + u, 32, stride=20), :] for u in range(5)]
+        rolled = [pltpu.roll(q, 64, 1) for q in pick]
+        for f in range(2):
+            at = (2 * g + f) * 128
+            out_ref[pl.ds(at, 32, stride=2), :] = jnp.where(left, pick[3 * f], rolled[3 * f + 1])
+            out_ref[pl.ds(at + 1, 32, stride=2), :] = pltpu.roll(pick[2], 96, 1) if f else pick[2]
+            out_ref[pl.ds(at + 64, 32, stride=2), :] = backwards(
+                jnp.where(left, rolled[3 * f], pick[3 * f + 1])
+            )
+            out_ref[pl.ds(at + 65, 32, stride=2), :] = backwards(
+                pltpu.roll(pick[2], 32, 1) if f else rolled[2]
+            )
 
 
 def circle(degrees):
@@ -242,26 +251,29 @@
     out_ref[pl.ds(1, SLOTS, stride=2), 0:32] = sent[128:].T
 
 
-def analysis_kernel(pairs_ref, in_ref, table_ref, out_ref, turned, south):
-    for block in range(32):
-        at = (63 - block) * 16
-        south[block * 16 : block * 16 + 16, :] = in_ref[at : at + 16, :]
-    lane = lax.broadcasted_iota(jnp.int32, (128, 128), 1)
+def analysis_kernel(pairs_ref, in_ref, table_ref, out_ref, turned):
+    lane = lax.broadcasted_iota(jnp.int32, (32, 128), 1)
     left = lane < 64
-    north_a, north_b = ([in_ref[pl.ds(2 * f + c, 128, stride=4), :] for f in range(2)] for c in range(2))
-    south_a, south_b = ([south[pl.ds(2 * f + c, 128, stride=4), :] for f in range(2)] for c in range(2))
-    for f in range(2):
-        turned[pl.ds(3 * f, 128, stride=5), :] = jnp.where(
-            left, north_a[f], pltpu.roll(south_a[f], 64, 1)
+    for g in range(4):
+        shared = []
+        for f in range(2):
+            at = (2 * g + f) * 128
+            north, north_last = (in_ref[pl.ds(at + c, 32, stride=2), :] for c in range(2))
+            south, south_last = (
+                backwards(in_ref[pl.ds(at + 64 + c, 32, stride=2), :]) for c in range(2)
+            )
+            turned[pl.ds(5 * g + 3 * f, 32, stride=20), :] = jnp.where(
+                left, north, pltpu.roll(south, 64, 1)
+            )
+            turned[pl.ds(5 * g + 3 * f + 1, 32, stride=20), :] = jnp.where(
+                left, pltpu.roll(north, 64, 1), south
+            )
+            shared += [north_last, south_last]
+        turned[pl.ds(5 * g + 2, 32, stride=20), :] = jnp.where(
+            left,
+            jnp.where(lane < 32, shared[0], pltpu.roll(shared[2], 32, 1)),
+            jnp.where(lane < 96, pltpu.roll(shared[1], 64, 1), pltpu.roll(shared[3], 96, 1)),
         )
-        turned[pl.ds(3 * f + 1, 128, stride=5), :] = jnp.where(
-            left, pltpu.roll(north_a[f], 64, 1), south_a[f]
-        )
-    turned[pl.ds(2, 128, stride=5), :] = jnp.where(
-        left,
-        jnp.where(lane < 32, north_b[0], pltpu.roll(north_b[1], 32, 1)),
-        jnp.where(lane < 96, pltpu.roll(south_b[0], 64, 1), pltpu.roll(south_b[1], 96, 1)),
-    )
     straight = turned[...].T
     north, south_rows = straight[:64], straight[64:]
     table_high, table_low = split(table_ref[0])
@@ -325,7 +337,6 @@
         out_specs=VMEM,
         scratch_shapes=[
             pltpu.VMEM((HALF, 128), F32),
-            pltpu.VMEM((SLOTS, 128), F32),
         ],
         compiler_params=PARAMS,
         name="legendre_synthesis",
@@ -355,7 +366,7 @@
         out_shape=jax.ShapeDtypeStruct((1, 32, ROWS), F32),
         in_specs=[VMEM] * 3,
         out_specs=VMEM,
-        scratch_shapes=[pltpu.VMEM((HALF, 128), F32), pltpu.VMEM((SLOTS, 128), F32)],
+        scratch_shapes=[pltpu.VMEM((HALF, 128), F32)],
         compiler_params=PARAMS,
         name="legendre_analysis",
     )(slot_pair.reshape(-1, 128), returned, leg_analysis)
@@ -363,7 +374,7 @@
 
 def exchange(messages):
     return lax.all_to_all(
-        messages.reshape(SLOTS, 2, 128), ("band", "lon"), split_axis=0, concat_axis=0, tiled=True
+        messages.reshape(SLOTS, 2, 128), ("lon", "band"), split_axis=0, concat_axis=0, tiled=True
     ).reshape(2 * SLOTS, 128)
 
 
@@ -371,7 +382,8 @@
     spectral_in, leg_synthesis, leg_analysis, slot_pair, departure_cells, departure_frac
 ):
     arrived = exchange(legendre_synthesis(slot_pair, spectral_in, leg_synthesis))
-    choice = slot_choice(slot_pair)
+    lons = lax.axis_size("lon")
+    choice = slot_choice(slot_pair.reshape(-1, lons).T.reshape(-1))
     weights = advection_weights(
         departure_cells, departure_frac, lax.axis_index("band"), lax.axis_index("lon"),
         lax.axis_size("band"),

time: 85.2 us -> 84.3 us (0.989)
  no operation moved by 1% of the time
where the time goes in v4:
time: 84.3 us; the launch traced here: 84.1 us
  waiting for transfers between devices  39.4 us (47%)
  starting transfers between devices  30.5 us (36%)
  Pallas kernels  7.03 us (8%)
  local copies, waits for them, and re-layouts  6.44 us (8%)
    all_to_all x2, waiting for transfers between devices, exchange(): lax.all_to_all(messages.reshape(SLOTS, 2, 128), ('lon', 'band'), split_ax...  39.4 us
    all_to_all x2, starting transfers between devices, exchange(): lax.all_to_all(messages.reshape(SLOTS, 2, 128), ('lon', 'band'), split_ax...  30.5 us
    unnamed x16, local copies, waits for them, and re-layouts  5.08 us
    pallas_call x1, Pallas kernels, grid_step(): pl.pallas_call(grid_kernel, out_shape=jax.ShapeDtypeStruct((2 * SLOTS, 12...  3.55 us
    pallas_call x1, Pallas kernels, legendre_synthesis(): pl.pallas_call(synthesis_kernel, out_shape=jax.ShapeDtypeStruct((2 * SLOT...  1.84 us
  transfers between devices with their start and end apart: 2, of which 2 were waited for; matrix products, arithmetic and copies ran while one was open for 6% of the time, Pallas kernels for 0%

profile of v4, /device:TPU:1, one launch (start us, length us, event | category | flops | bytes accessed | tf_op | source)
XLA Modules:
  0.0 84.1 jit_solution(9622185798934618095)
XLA Ops:
  0.0 0.0 copy-start
  0.0 1.6 %copy.12.table_ref = f32[1,641,640]{2,1,0:T(8,128)S(1)} copy(f32[1,641,640]{2,0,1:T(1,128)} %param.10) | data formatting | bytes 3281920 | tf_op args[1]
  1.6 0.0 copy-done.5
  1.6 0.0 copy-start.6
  1.6 1.8 %legendre_synthesis.1 = f32[1024,128]{1,0:T(8,128)} custom-call(s32[4,128]{1,0:T(4,128)S(1)} %bitcast.10, f32[1,32,641]{2,1,0:T(8,128)S(1)} %copy-done.3, f32[1,641,640]{2,1,0:T(8,128)S(1)} %copy.12.table_ref), custom_call_target="tpu_custom_call" | custom-call | tf_op jit(solution)/shard_map/legendre_synthesis/pallas_call | solution.py:333
  3.5 22.2 %all-to-all-start = ((f32[512,2,128]{2,1,0:T(2,128)}), f32[512,2,128]{2,1,0:T(2,128)S(1)}, u32[]{:S(2)}, u32[]{:S(2)}) async-start(f32[512,2,128]{2,1,0:T(2,128)} %bitcast.1), calls=%async_computation | async-start | bytes 1048576 | tf_op jit(solution)/shard_map/all_to_all | solution.py:376
  25.7 0.0 copy-start.1
  25.8 0.0 copy-start.2
  25.8 0.0 copy-start.4
  25.8 0.6 gather_fusion.1
  26.4 0.6 gather_fusion
  26.9 0.1 broadcast_subtract_fusion
  27.0 0.1 broadcast_select_fusion.1
  27.1 0.1 reshape.189
  27.2 0.1 copy.13
  27.3 0.1 eq.26
  27.3 0.2 compare_convert_fusion.choice_ref
  27.5 0.2 select_add_fusion.weight_ref
  27.7 20.4 %all-to-all-done = f32[512,2,128]{2,1,0:T(2,128)S(1)} async-done(((f32[512,2,128]{2,1,0:T(2,128)}), f32[512,2,128]{2,1,0:T(2,128)S(1)}, u32[]{:S(2)}, u32[]{:S(2)}) %all-to-all-start) | async-done | bytes 524320 | tf_op jit(solution)/shard_map/all_to_all | solution.py:376
  48.1 3.5 %grid_step.1 = f32[1024,128]{1,0:T(8,128)} custom-call(f32[1024,128]{1,0:T(8,128)S(1)} %bitcast.8, bf16[512,640]{1,0:T(8,128)(2,1)S(1)} %compare_convert_fusion.choice_ref, f32[5,5,2560]{2,1,0:T(8,128)S(1)} %select_add_fusion.weight_ref, bf16[384,512]{1,0:T(8,128)(2,1)S(1)} %copy-done.1, bf16[512,256]{1,0:T(8,128)(2,1)S(1)} %copy-done.2, f32[20,256]{1,0:T(8,128)S(1)} %copy-done.4), custom_call_target="tpu_custom_call" | custom-call | tf_op jit(solution)/shard_map/grid_step/pallas_call | solution.py:347
  51.7 8.3 %all-to-all-start.1 = ((f32[512,2,128]{2,1,0:T(2,128)}), f32[512,2,128]{2,1,0:T(2,128)S(1)}, u32[]{:S(2)}, u32[]{:S(2)}) async-start(f32[512,2,128]{2,1,0:T(2,128)} %bitcast.5), calls=%async_computation.1 | async-start | bytes 1048576 | tf_op jit(solution)/shard_map/all_to_all | solution.py:376
  60.0 3.5 %copy.14.table_ref = f32[1,640,641]{2,1,0:T(8,128)S(1)} copy(f32[1,640,641]{1,0,2:T(1,128)} %param.11) | data formatting | bytes 3281920 | tf_op args[2]
  63.5 18.9 %all-to-all-done.1 = f32[512,2,128]{2,1,0:T(2,128)S(1)} async-done(((f32[512,2,128]{2,1,0:T(2,128)}), f32[512,2,128]{2,1,0:T(2,128)S(1)}, u32[]{:S(2)}, u32[]{:S(2)}) %all-to-all-start.1) | async-done | bytes 524320 | tf_op jit(solution)/shard_map/all_to_all | solution.py:376
  82.4 1.6 %legendre_analysis.1 = f32[1,32,641]{2,1,0:T(8,128)} custom-call(s32[4,128]{1,0:T(4,128)S(1)} %bitcast.11, f32[1024,128]{1,0:T(8,128)S(1)} %bitcast.9, f32[1,640,641]{2,1,0:T(8,128)S(1)} %copy.14.table_ref), custom_call_target="tpu_custom_call" | custom-call | tf_op jit(solution)/shard_map/legendre_analysis/pallas_call | solution.py:364
  (13 shorter events, 0.1 us)
Async XLA Ops:
  0.0 25.7 %copy-start = (f32[20,2560]{1,0:T(8,128)S(1)}, f32[20,2560]{1,0:T(8,128)}, u32[]{:S(2)}) copy-start(f32[20,2560]{1,0:T(8,128)} %param.14) | copy-start | bytes 614404
  0.0 1.6 %copy-start.5 = (s32[512]{0:T(512)S(1)}, s32[512]{0:T(512)}, u32[]{:S(2)}) copy-start(s32[512]{0:T(512)} %param.12) | copy-start | bytes 6148
  0.0 1.6 %copy-start.3 = (f32[1,32,641]{2,1,0:T(8,128)S(1)}, f32[1,32,641]{2,1,0:T(8,128)}, u32[]{:S(2)}) copy-start(f32[1,32,641]{2,1,0:T(8,128)} %spec_ref.1) | copy-start | bytes 246148
  1.6 24.7 %copy-start.6 = (s32[20,2560]{1,0:T(8,128)S(1)}, s32[20,2560]{1,0:T(8,128)}, u32[]{:S(2)}) copy-start(s32[20,2560]{1,0:T(8,128)} %param.13) | copy-start | bytes 614404
  3.5 44.6 %all-to-all-start = ((f32[512,2,128]{2,1,0:T(2,128)}), f32[512,2,128]{2,1,0:T(2,128)S(1)}, u32[]{:S(2)}, u32[]{:S(2)}) async-start(f32[512,2,128]{2,1,0:T(2,128)} %bitcast.1), calls=%async_computation | async-start | bytes 1048576 | tf_op jit(solution)/shard_map/all_to_all | solution.py:376
  25.7 22.4 %copy-start.1 = (bf16[384,512]{1,0:T(8,128)(2,1)S(1)}, bf16[384,512]{1,0:T(8,128)(2,1)}, u32[]{:S(2)}) copy-start(bf16[384,512]{1,0:T(8,128)(2,1)} %constant.123.clone.synth_ref) | copy-start | bytes 1179652
  25.8 22.4 %copy-start.2 = (bf16[512,256]{1,0:T(8,128)(2,1)S(1)}, bf16[512,256]{1,0:T(8,128)(2,1)}, u32[]{:S(2)}) copy-start(bf16[512,256]{1,0:T(8,128)(2,1)} %constant.124.clone.anal_ref) | copy-start | bytes 786436
  25.8 22.4 %copy-start.4 = (f32[20,256]{1,0:T(8,128)S(1)}, f32[20,256]{1,0:T(8,128)}, u32[]{:S(2)}) copy-start(f32[20,256]{1,0:T(8,128)} %constant.125.clone.twiddle_ref) | copy-start | bytes 61444
  51.7 30.7 %all-to-all-start.1 = ((f32[512,2,128]{2,1,0:T(2,128)}), f32[512,2,128]{2,1,0:T(2,128)S(1)}, u32[]{:S(2)}, u32[]{:S(2)}) async-start(f32[512,2,128]{2,1,0:T(2,128)} %bitcast.5), calls=%async_computation.1 | async-start | bytes 1048576 | tf_op jit(solution)/shard_map/all_to_all | solution.py:376

commit v5 on v4

--- a/solution.py
+++ b/solution.py
@@ -87,7 +87,12 @@
     return jnp.concatenate(parts, axis=0)
 
 
-def synthesis_kernel(pairs_ref, spec_ref, table_ref, out_ref, turned):
+def leave(built, out_hbm, sent, n):
+    rows = pl.ds(n * 256, 256)
+    return pltpu.make_async_copy(built.at[rows, :], out_hbm.at[rows, :], sent.at[n])
+
+
+def synthesis_kernel(pairs_ref, spec_ref, table_ref, out_hbm, turned, out_ref, sent):
     pair = own_pair(pairs_ref)
     upper, odd = wave_rows(pair)
     live = pair < PAIRS
@@ -119,6 +124,9 @@
             out_ref[pl.ds(at + 65, 32, stride=2), :] = backwards(
                 pltpu.roll(pick[2], 32, 1) if f else rolled[2]
             )
+        leave(out_ref, out_hbm, sent, g).start()
+    for g in range(4):
+        leave(out_ref, out_hbm, sent, g).wait()
 
 
 def circle(degrees):
@@ -159,8 +167,8 @@
 
 
 def grid_kernel(
-    in_ref, choice_ref, weight_ref, synth_ref, anal_ref, twiddle_ref, out_ref,
-    coeff, spread, fields, back
+    in_ref, choice_ref, weight_ref, synth_ref, anal_ref, twiddle_ref, out_hbm,
+    coeff, spread, fields, back, out_ref, left_core
 ):
     columns = jnp.concatenate(
         [in_ref[pl.ds(0, SLOTS, stride=2), :].T, in_ref[pl.ds(1, SLOTS, stride=2), :].T[:32]], axis=0
@@ -207,9 +215,10 @@
             real.append(tr * zr - ti * zi)
             imag.append(None if r == 5 else tr * zi + ti * zr)
         value = jnp.concatenate(to_segments(real, imag), axis=1)
-        moved = weight_ref[i, 0:1, :] * value
-        for offset in range(1, REACH + 1):
-            moved = moved + weight_ref[i, offset : offset + 1, :] * pltpu.roll(value, offset, 1)
+        behind = pltpu.roll(value, 1, 1)
+        w = [weight_ref[i, n : n + 1, :] for n in range(REACH + 1)]
+        inner = w[2] * value + w[3] * behind + pltpu.roll(w[4] * value, 2, 1)
+        moved = w[0] * value + w[1] * behind + pltpu.roll(inner, 2, 1)
         waves = from_segments([moved[:, k * SEG : k * SEG + SEG] for k in range(RADIX)])
         for r in range(RADIX):
             vr, vi = waves[r] if r < 6 else waves[RADIX - r]
@@ -247,8 +256,13 @@
         preferred_element_type=F32,
     )
     sent = sent[:160] + sent[160:]
-    out_ref[pl.ds(0, SLOTS, stride=2), :] = sent[:128].T
-    out_ref[pl.ds(1, SLOTS, stride=2), 0:32] = sent[128:].T
+    for n in range(4):
+        block = sent[:, n * 128 : n * 128 + 128]
+        out_ref[pl.ds(n * 256, 128, stride=2), :] = block[:128].T
+        out_ref[pl.ds(n * 256 + 1, 128, stride=2), 0:32] = block[128:].T
+        leave(out_ref, out_hbm, left_core, n).start()
+    for n in range(4):
+        leave(out_ref, out_hbm, left_core, n).wait()
 
 
 def analysis_kernel(pairs_ref, in_ref, table_ref, out_ref, turned):
@@ -306,6 +320,7 @@
 
 
 VMEM = pl.BlockSpec(memory_space=pltpu.VMEM)
+HBM = pl.BlockSpec(memory_space=pltpu.HBM)
 PARAMS = pltpu.CompilerParams(vmem_limit_bytes=40 * 1024 * 1024)
 
 
@@ -324,8 +339,12 @@
     cells = jnp.take(cells, row, axis=0)[:, None, :]
     fraction = jnp.take(fraction, row, axis=0)[:, None, :]
     offset = jnp.arange(REACH + 1, dtype=jnp.int32)[None, :, None]
-    return jnp.where(cells == offset, 1.0 - fraction, 0.0) + jnp.where(
+    weight = jnp.where(cells == offset, 1.0 - fraction, 0.0) + jnp.where(
         cells == offset - 1, fraction, 0.0
+    )
+    return jnp.concatenate(
+        [weight[:, :2], jnp.roll(weight[:, 2:4], -2, axis=2), jnp.roll(weight[:, 4:], -4, axis=2)],
+        axis=1,
     )
 
 
@@ -334,9 +353,11 @@
         synthesis_kernel,
         out_shape=jax.ShapeDtypeStruct((2 * SLOTS, 128), F32),
         in_specs=[VMEM] * 3,
-        out_specs=VMEM,
+        out_specs=HBM,
         scratch_shapes=[
             pltpu.VMEM((HALF, 128), F32),
+            pltpu.VMEM((2 * SLOTS, 128), F32),
+            pltpu.SemaphoreType.DMA((4,)),
         ],
         compiler_params=PARAMS,
         name="legendre_synthesis",
@@ -348,12 +369,14 @@
         grid_kernel,
         out_shape=jax.ShapeDtypeStruct((2 * SLOTS, 128), F32),
         in_specs=[VMEM] * 6,
-        out_specs=VMEM,
+        out_specs=HBM,
         scratch_shapes=[
             pltpu.VMEM((400, 256), F32),
             pltpu.VMEM((400, 2 * SEG), F32),
             pltpu.VMEM((400, 2 * SEG), F32),
             pltpu.VMEM((160, WAVES), F32),
+            pltpu.VMEM((2 * SLOTS, 128), F32),
+            pltpu.SemaphoreType.DMA((4,)),
         ],
         compiler_params=PARAMS,
         name="grid_step",

time: 84.3 us -> 84.3 us (level)
  transfers between devices with their start and end apart: 2 -> 2, of which waited for: 2 -> 2; matrix products, arithmetic and copies ran while one was open for 6% -> 7% of each run, Pallas kernels for 0% -> 0%
where the time goes in v5:
time: 84.3 us; the launch traced here: 84 us
  waiting for transfers between devices  38.8 us (46%)
  starting transfers between devices  30.5 us (36%)
  Pallas kernels  6.94 us (8%)
  local copies, waits for them, and re-layouts  6.84 us (8%)
    all_to_all x2, waiting for transfers between devices, exchange(): lax.all_to_all(messages.reshape(SLOTS, 2, 128), ('lon', 'band'), split_ax...  38.8 us
    all_to_all x2, starting transfers between devices, exchange(): lax.all_to_all(messages.reshape(SLOTS, 2, 128), ('lon', 'band'), split_ax...  30.5 us
    unnamed x16, local copies, waits for them, and re-layouts  5.08 us
    pallas_call x1, Pallas kernels, grid_step(): pl.pallas_call(grid_kernel, out_shape=jax.ShapeDtypeStruct((2 * SLOTS, 12...  3.47 us
    pallas_call x1, Pallas kernels, legendre_synthesis(): pl.pallas_call(synthesis_kernel, out_shape=jax.ShapeDtypeStruct((2 * SLOT...  1.83 us
  transfers between devices with their start and end apart: 2, of which 2 were waited for; matrix products, arithmetic and copies ran while one was open for 7% of the time, Pallas kernels for 0%

profile of v5, /device:TPU:1, one launch (start us, length us, event | category | flops | bytes accessed | tf_op | source)
XLA Modules:
  0.0 84.0 jit_solution(16812953265191837173)
XLA Ops:
  0.0 1.6 %copy.12.table_ref = f32[1,641,640]{2,1,0:T(8,128)S(1)} copy(f32[1,641,640]{2,0,1:T(1,128)} %param.10) | data formatting | bytes 3281920 | tf_op args[1]
  1.6 1.8 %legendre_synthesis.1 = f32[1024,128]{1,0:T(8,128)} custom-call(s32[4,128]{1,0:T(4,128)S(1)} %bitcast.10, f32[1,32,641]{2,1,0:T(8,128)S(1)} %copy-done.3, f32[1,641,640]{2,1,0:T(8,128)S(1)} %copy.12.table_ref), custom_call_target="tpu_custom_call" | custom-call | tf_op jit(solution)/shard_map/legendre_synthesis/pallas_call | solution.py:352
  3.5 22.2 %all-to-all-start = ((f32[512,2,128]{2,1,0:T(2,128)}), f32[512,2,128]{2,1,0:T(2,128)S(1)}, u32[]{:S(2)}, u32[]{:S(2)}) async-start(f32[512,2,128]{2,1,0:T(2,128)} %bitcast.1), calls=%async_computation | async-start | bytes 1048576 | tf_op jit(solution)/shard_map/all_to_all | solution.py:399
  25.8 0.6 gather_fusion.1
  26.3 0.6 gather_fusion
  26.9 0.0 copy-start.1
  26.9 0.0 copy-start.2
  26.9 0.0 copy-start.4
  27.0 0.1 broadcast_subtract_fusion
  27.0 0.1 broadcast_select_fusion.1
  27.1 0.2 select_add_fusion
  27.3 0.1 reshape.189
  27.4 0.2 slice.37
  27.6 0.2 slice.35
  27.8 0.1 copy.13
  27.9 0.1 eq.26
  27.9 0.2 compare_convert_fusion.choice_ref
  28.1 0.1 fusion.weight_ref
  28.3 19.8 %all-to-all-done = f32[512,2,128]{2,1,0:T(2,128)S(1)} async-done(((f32[512,2,128]{2,1,0:T(2,128)}), f32[512,2,128]{2,1,0:T(2,128)S(1)}, u32[]{:S(2)}, u32[]{:S(2)}) %all-to-all-start) | async-done | bytes 524320 | tf_op jit(solution)/shard_map/all_to_all | solution.py:399
  48.1 3.5 %grid_step.1 = f32[1024,128]{1,0:T(8,128)} custom-call(f32[1024,128]{1,0:T(8,128)S(1)} %bitcast.8, bf16[512,640]{1,0:T(8,128)(2,1)S(1)} %compare_convert_fusion.choice_ref, f32[5,5,2560]{2,1,0:T(8,128)S(1)} %fusion.weight_ref, bf16[384,512]{1,0:T(8,128)(2,1)S(1)} %copy-done.1, bf16[512,256]{1,0:T(8,128)(2,1)S(1)} %copy-done.2, f32[20,256]{1,0:T(8,128)S(1)} %copy-done.4), custom_call_target="tpu_custom_call" | custom-call | tf_op jit(solution)/shard_map/grid_step/pallas_call | solution.py:368
  51.6 8.3 %all-to-all-start.1 = ((f32[512,2,128]{2,1,0:T(2,128)}), f32[512,2,128]{2,1,0:T(2,128)S(1)}, u32[]{:S(2)}, u32[]{:S(2)}) async-start(f32[512,2,128]{2,1,0:T(2,128)} %bitcast.5), calls=%async_computation.1 | async-start | bytes 1048576 | tf_op jit(solution)/shard_map/all_to_all | solution.py:399
  60.0 3.5 %copy.14.table_ref = f32[1,640,641]{2,1,0:T(8,128)S(1)} copy(f32[1,640,641]{1,0,2:T(1,128)} %param.11) | data formatting | bytes 3281920 | tf_op args[2]
  63.4 18.9 %all-to-all-done.1 = f32[512,2,128]{2,1,0:T(2,128)S(1)} async-done(((f32[512,2,128]{2,1,0:T(2,128)}), f32[512,2,128]{2,1,0:T(2,128)S(1)}, u32[]{:S(2)}, u32[]{:S(2)}) %all-to-all-start.1) | async-done | bytes 524320 | tf_op jit(solution)/shard_map/all_to_all | solution.py:399
  82.4 1.6 %legendre_analysis.1 = f32[1,32,641]{2,1,0:T(8,128)} custom-call(s32[4,128]{1,0:T(4,128)S(1)} %bitcast.11, f32[1024,128]{1,0:T(8,128)S(1)} %bitcast.9, f32[1,640,641]{2,1,0:T(8,128)S(1)} %copy.14.table_ref), custom_call_target="tpu_custom_call" | custom-call | tf_op jit(solution)/shard_map/legendre_analysis/pallas_call | solution.py:387
  (19 shorter events, 0.1 us)
Async XLA Ops:
  0.0 25.7 %copy-start = (f32[20,2560]{1,0:T(8,128)S(1)}, f32[20,2560]{1,0:T(8,128)}, u32[]{:S(2)}) copy-start(f32[20,2560]{1,0:T(8,128)} %param.14) | copy-start | bytes 614404
  0.0 1.6 %copy-start.5 = (s32[512]{0:T(512)S(1)}, s32[512]{0:T(512)}, u32[]{:S(2)}) copy-start(s32[512]{0:T(512)} %param.12) | copy-start | bytes 6148
  0.0 1.6 %copy-start.3 = (f32[1,32,641]{2,1,0:T(8,128)S(1)}, f32[1,32,641]{2,1,0:T(8,128)}, u32[]{:S(2)}) copy-start(f32[1,32,641]{2,1,0:T(8,128)} %spec_ref.1) | copy-start | bytes 246148
  1.6 24.7 %copy-start.6 = (s32[20,2560]{1,0:T(8,128)S(1)}, s32[20,2560]{1,0:T(8,128)}, u32[]{:S(2)}) copy-start(s32[20,2560]{1,0:T(8,128)} %param.13) | copy-start | bytes 614404
  3.5 44.7 %all-to-all-start = ((f32[512,2,128]{2,1,0:T(2,128)}), f32[512,2,128]{2,1,0:T(2,128)S(1)}, u32[]{:S(2)}, u32[]{:S(2)}) async-start(f32[512,2,128]{2,1,0:T(2,128)} %bitcast.1), calls=%async_computation | async-start | bytes 1048576 | tf_op jit(solution)/shard_map/all_to_all | solution.py:399
  26.9 21.2 %copy-start.1 = (bf16[384,512]{1,0:T(8,128)(2,1)S(1)}, bf16[384,512]{1,0:T(8,128)(2,1)}, u32[]{:S(2)}) copy-start(bf16[384,512]{1,0:T(8,128)(2,1)} %constant.123.clone.synth_ref) | copy-start | bytes 1179652
  26.9 21.2 %copy-start.2 = (bf16[512,256]{1,0:T(8,128)(2,1)S(1)}, bf16[512,256]{1,0:T(8,128)(2,1)}, u32[]{:S(2)}) copy-start(bf16[512,256]{1,0:T(8,128)(2,1)} %constant.124.clone.anal_ref) | copy-start | bytes 786436
  26.9 21.2 %copy-start.4 = (f32[20,256]{1,0:T(8,128)S(1)}, f32[20,256]{1,0:T(8,128)}, u32[]{:S(2)}) copy-start(f32[20,256]{1,0:T(8,128)} %constant.125.clone.twiddle_ref) | copy-start | bytes 61444
  51.6 30.8 %all-to-all-start.1 = ((f32[512,2,128]{2,1,0:T(2,128)}), f32[512,2,128]{2,1,0:T(2,128)S(1)}, u32[]{:S(2)}, u32[]{:S(2)}) async-start(f32[512,2,128]{2,1,0:T(2,128)} %bitcast.5), calls=%async_computation.1 | async-start | bytes 1048576 | tf_op jit(solution)/shard_map/all_to_all | solution.py:399

commit v6 on v5

--- a/solution.py
+++ b/solution.py
@@ -92,7 +92,29 @@
     return pltpu.make_async_copy(built.at[rows, :], out_hbm.at[rows, :], sent.at[n])
 
 
-def synthesis_kernel(pairs_ref, spec_ref, table_ref, out_hbm, turned, out_ref, sent):
+CUTS = ((0, 384), (384, ROWS - 384))
+LANES = HALF // 128
+
+
+def synthesis_kernel(
+    pairs_hbm, spec_hbm, table_hbm, out_hbm, pairs_ref, spec_ref, table, turned, out_ref, arrived, sent
+):
+    small = [
+        pltpu.make_async_copy(pairs_hbm, pairs_ref, arrived.at[0]),
+        pltpu.make_async_copy(spec_hbm, spec_ref, arrived.at[1]),
+    ]
+    large = [
+        pltpu.make_async_copy(
+            table_hbm.at[pl.ds(LANES * first, LANES * rows), 0, :],
+            table.at[pl.ds(LANES * first, LANES * rows), :],
+            arrived.at[2 + n],
+        )
+        for n, (first, rows) in enumerate(CUTS)
+    ]
+    for copy in large[:1] + small + large[1:]:
+        copy.start()
+    for copy in small:
+        copy.wait()
     pair = own_pair(pairs_ref)
     upper, odd = wave_rows(pair)
     live = pair < PAIRS
@@ -105,8 +127,14 @@
                 for part in range(2):
                     first = part * 16 + half * 8
                     groups.append(jnp.where(mask, spec_ref[0, first : first + 8, :], 0.0))
-    table_high, table_low = split(table_ref[0])
-    product = dot3(jnp.concatenate(groups, axis=0), table_high, table_low)
+    masked = jnp.concatenate(groups, axis=0)
+    product = jnp.zeros((128, HALF), F32)
+    for copy, (first, rows) in zip(large, CUTS):
+        copy.wait()
+        block = jnp.concatenate(
+            [table[pl.ds(LANES * first + n, rows, stride=LANES), :] for n in range(LANES)], axis=1
+        )
+        product = product + dot3(masked[:, first : first + rows], *split(block))
     even, odd_sum = product[:64], product[64:]
     turned[...] = jnp.concatenate([even + odd_sum, even - odd_sum], axis=0).T
     lane = lax.broadcasted_iota(jnp.int32, (32, 128), 1)
@@ -349,19 +377,24 @@
 
 
 def legendre_synthesis(slot_pair, spectral_in, leg_synthesis):
+    pairs = slot_pair.reshape(-1, 128)
     return pl.pallas_call(
         synthesis_kernel,
         out_shape=jax.ShapeDtypeStruct((2 * SLOTS, 128), F32),
-        in_specs=[VMEM] * 3,
+        in_specs=[HBM] * 3,
         out_specs=HBM,
         scratch_shapes=[
+            pltpu.VMEM(pairs.shape, jnp.int32),
+            pltpu.VMEM(spectral_in.shape, F32),
+            pltpu.VMEM((3208, 128), F32),
             pltpu.VMEM((HALF, 128), F32),
             pltpu.VMEM((2 * SLOTS, 128), F32),
+            pltpu.SemaphoreType.DMA((2 + len(CUTS),)),
             pltpu.SemaphoreType.DMA((4,)),
         ],
-        compiler_params=PARAMS,
+        compiler_params=pltpu.CompilerParams(vmem_limit_bytes=60 * 1024 * 1024),
         name="legendre_synthesis",
-    )(slot_pair.reshape(-1, 128), spectral_in, leg_synthesis)
+    )(pairs, spectral_in, leg_synthesis.reshape(ROWS * LANES, 1, 128))
 
 
 def grid_step(arrived, choice, weights):

time: 84.3 us -> 84.1 us (level)
  local copies, waits for them, and re-layouts: 6.84 us -> 5.25 us
  Pallas kernels: 6.94 us -> 8.51 us
    unnamed x16 -> x13, local copies, waits for them, and re-layouts: 5.08 us -> 3.49 us
    pallas_call x1, Pallas kernels: 1.83 us -> 3.39 us  [legendre_synthesis(): pl.pallas_call(synthesis_kernel, out_shape=jax.ShapeDtypeStruct((2 * SLOT...]
where the time goes in v6:
time: 84.1 us; the launch traced here: 83.9 us
  waiting for transfers between devices  38.6 us (46%)
  starting transfers between devices  30.5 us (36%)
  Pallas kernels  8.51 us (10%)
  local copies, waits for them, and re-layouts  5.25 us (6%)
    all_to_all x2, waiting for transfers between devices, exchange(): lax.all_to_all(messages.reshape(SLOTS, 2, 128), ('lon', 'band'), split_ax...  38.6 us
    all_to_all x2, starting transfers between devices, exchange(): lax.all_to_all(messages.reshape(SLOTS, 2, 128), ('lon', 'band'), split_ax...  30.5 us
    unnamed x13, local copies, waits for them, and re-layouts  3.49 us
    pallas_call x1, Pallas kernels, grid_step(): pl.pallas_call(grid_kernel, out_shape=jax.ShapeDtypeStruct((2 * SLOTS, 12...  3.47 us
    pallas_call x1, Pallas kernels, legendre_synthesis(): pl.pallas_call(synthesis_kernel, out_shape=jax.ShapeDtypeStruct((2 * SLOT...  3.39 us
  transfers between devices with their start and end apart: 2, of which 2 were waited for; matrix products, arithmetic and copies ran while one was open for 7% of the time, Pallas kernels for 0%

profile of v6, /device:TPU:1, one launch (start us, length us, event | category | flops | bytes accessed | tf_op | source)
XLA Modules:
  0.0 83.9 jit_solution(8025987891626952315)
XLA Ops:
  0.0 3.4 %legendre_synthesis.1 = f32[1024,128]{1,0:T(8,128)} custom-call(s32[4,128]{1,0:T(4,128)} %bitcast.11, f32[1,32,641]{2,1,0:T(8,128)} %spec_hbm.1, f32[3205,1,128]{2,1,0:T(1,128)} %bitcast.14), custom_call_target="tpu_custom_call" | custom-call | tf_op jit(solution)/shard_map/legendre_synthesis/pallas_call | solution.py:381
  3.4 0.0 copy-start.4
  3.4 22.2 %all-to-all-start = ((f32[512,2,128]{2,1,0:T(2,128)}), f32[512,2,128]{2,1,0:T(2,128)S(1)}, u32[]{:S(2)}, u32[]{:S(2)}) async-start(f32[512,2,128]{2,1,0:T(2,128)} %bitcast.13), calls=%async_computation | async-start | bytes 1048576 | tf_op jit(solution)/shard_map/all_to_all | solution.py:432
  25.7 0.6 gather_fusion.1
  26.3 0.6 gather_fusion
  26.9 0.0 copy-start.1
  26.9 0.0 copy-start.2
  26.9 0.0 copy-start.3
  26.9 0.1 broadcast_select_fusion.1
  27.0 0.1 broadcast_subtract_fusion
  27.1 0.2 select_add_fusion
  27.2 0.1 reshape.193
  27.4 0.2 slice.37
  27.5 0.2 slice.35
  27.8 0.1 copy.11
  27.8 0.1 eq.26
  27.9 0.2 compare_convert_fusion.choice_ref
  28.1 0.1 fusion.weight_ref
  28.3 19.7 %all-to-all-done = f32[512,2,128]{2,1,0:T(2,128)S(1)} async-done(((f32[512,2,128]{2,1,0:T(2,128)}), f32[512,2,128]{2,1,0:T(2,128)S(1)}, u32[]{:S(2)}, u32[]{:S(2)}) %all-to-all-start) | async-done | bytes 524320 | tf_op jit(solution)/shard_map/all_to_all | solution.py:432
  48.0 3.5 %grid_step.1 = f32[1024,128]{1,0:T(8,128)} custom-call(f32[1024,128]{1,0:T(8,128)S(1)} %bitcast.9, bf16[512,640]{1,0:T(8,128)(2,1)S(1)} %compare_convert_fusion.choice_ref, f32[5,5,2560]{2,1,0:T(8,128)S(1)} %fusion.weight_ref, bf16[384,512]{1,0:T(8,128)(2,1)S(1)} %copy-done.1, bf16[512,256]{1,0:T(8,128)(2,1)S(1)} %copy-done.2, f32[20,256]{1,0:T(8,128)S(1)} %copy-done.3), custom_call_target="tpu_custom_call" | custom-call | tf_op jit(solution)/shard_map/grid_step/pallas_call | solution.py:401
  51.5 8.4 %all-to-all-start.1 = ((f32[512,2,128]{2,1,0:T(2,128)}), f32[512,2,128]{2,1,0:T(2,128)S(1)}, u32[]{:S(2)}, u32[]{:S(2)}) async-start(f32[512,2,128]{2,1,0:T(2,128)} %bitcast.6), calls=%async_computation.1 | async-start | bytes 1048576 | tf_op jit(solution)/shard_map/all_to_all | solution.py:432
  59.8 3.5 %copy.12.table_ref = f32[1,640,641]{2,1,0:T(8,128)S(1)} copy(f32[1,640,641]{1,0,2:T(1,128)} %param.11) | data formatting | bytes 3281920 | tf_op args[2]
  63.3 18.9 %all-to-all-done.1 = f32[512,2,128]{2,1,0:T(2,128)S(1)} async-done(((f32[512,2,128]{2,1,0:T(2,128)}), f32[512,2,128]{2,1,0:T(2,128)S(1)}, u32[]{:S(2)}, u32[]{:S(2)}) %all-to-all-start.1) | async-done | bytes 524320 | tf_op jit(solution)/shard_map/all_to_all | solution.py:432
  82.2 1.6 %legendre_analysis.1 = f32[1,32,641]{2,1,0:T(8,128)} custom-call(s32[4,128]{1,0:T(4,128)S(1)} %bitcast.12, f32[1024,128]{1,0:T(8,128)S(1)} %bitcast.10, f32[1,640,641]{2,1,0:T(8,128)S(1)} %copy.12.table_ref), custom_call_target="tpu_custom_call" | custom-call | tf_op jit(solution)/shard_map/legendre_analysis/pallas_call | solution.py:420
  (16 shorter events, 0.1 us)
Async XLA Ops:
  0.0 25.7 %copy-start = (f32[20,2560]{1,0:T(8,128)S(1)}, f32[20,2560]{1,0:T(8,128)}, u32[]{:S(2)}) copy-start(f32[20,2560]{1,0:T(8,128)} %param.14) | copy-start | bytes 614404
  0.0 26.3 %copy-start.5 = (s32[20,2560]{1,0:T(8,128)S(1)}, s32[20,2560]{1,0:T(8,128)}, u32[]{:S(2)}) copy-start(s32[20,2560]{1,0:T(8,128)} %param.13) | copy-start | bytes 614404
  3.4 23.8 %copy-start.4 = (s32[512]{0:T(512)S(1)}, s32[512]{0:T(512)}, u32[]{:S(2)}) copy-start(s32[512]{0:T(512)} %param.12) | copy-start | bytes 6148
  3.4 44.6 %all-to-all-start = ((f32[512,2,128]{2,1,0:T(2,128)}), f32[512,2,128]{2,1,0:T(2,128)S(1)}, u32[]{:S(2)}, u32[]{:S(2)}) async-start(f32[512,2,128]{2,1,0:T(2,128)} %bitcast.13), calls=%async_computation | async-start | bytes 1048576 | tf_op jit(solution)/shard_map/all_to_all | solution.py:432
  26.9 21.1 %copy-start.1 = (bf16[384,512]{1,0:T(8,128)(2,1)S(1)}, bf16[384,512]{1,0:T(8,128)(2,1)}, u32[]{:S(2)}) copy-start(bf16[384,512]{1,0:T(8,128)(2,1)} %constant.123.clone.synth_ref) | copy-start | bytes 1179652
  26.9 21.1 %copy-start.2 = (bf16[512,256]{1,0:T(8,128)(2,1)S(1)}, bf16[512,256]{1,0:T(8,128)(2,1)}, u32[]{:S(2)}) copy-start(bf16[512,256]{1,0:T(8,128)(2,1)} %constant.124.clone.anal_ref) | copy-start | bytes 786436
  26.9 21.1 %copy-start.3 = (f32[20,256]{1,0:T(8,128)S(1)}, f32[20,256]{1,0:T(8,128)}, u32[]{:S(2)}) copy-start(f32[20,256]{1,0:T(8,128)} %constant.125.clone.twiddle_ref) | copy-start | bytes 61444
  51.5 30.8 %all-to-all-start.1 = ((f32[512,2,128]{2,1,0:T(2,128)}), f32[512,2,128]{2,1,0:T(2,128)S(1)}, u32[]{:S(2)}, u32[]{:S(2)}) async-start(f32[512,2,128]{2,1,0:T(2,128)} %bitcast.6), calls=%async_computation.1 | async-start | bytes 1048576 | tf_op jit(solution)/shard_map/all_to_all | solution.py:432
